TPU v7x, 256 devices: a whole 4x4x8 slice. The times are simulated.
256 devices in a mesh: row: 16 (over z, y_lo), col: 16 (over x, y_hi, core).
Axes of the slice: x: 4, y: 4 (y_hi: 2, y_lo: 2; y = y_hi * 2 + y_lo), z: 8, core: 2. Of those that a mesh axis runs over, the one named last changes fastest.
Arguments:
- features: bfloat16 [768, 8192], P('col', 'row'), may hold values from -6 to 6
- gate_weight: bfloat16 [8192, 14336], P('row', 'col'), may hold values from -0.0625 to 0.0625
- up_weight: bfloat16 [8192, 14336], P('row', 'col'), may hold values from -0.0625 to 0.0625
- down_weight: bfloat16 [14336, 8192], P('col', 'row'), may hold values from -0.046875 to 0.046875
- cotangent: bfloat16 [768, 8192], P('col', 'row'), may hold values from -6 to 6
Outputs:
- output: float32 [768, 8192], P('col', 'row')
- input_grad: float32 [768, 8192], P('col', 'row')
- gate_wgrad: float32 [8192, 14336], P('row', 'col')
- up_wgrad: float32 [8192, 14336], P('row', 'col')
- down_wgrad: float32 [14336, 8192], P('col', 'row')
All inputs are finite; a program needn't handle non-finite values.
Results may differ from a plain program's by a relative error of at most 0.0029.
Values may be sent and summed in bfloat16 or wider, within the bound.
A program may use at most 64 MiB of HBM per device.

v0:
```python
import jax
import jax.numpy as jnp
from jax import lax
from jax.sharding import PartitionSpec as P


def times_transposed(left, right):
    return lax.dot_general(
        left, right, (((1,), (1,)), ((), ())), preferred_element_type=jnp.float32
    )


def over_tokens(left, right):
    return lax.dot_general(
        left, right, (((0,), (0,)), ((), ())), preferred_element_type=jnp.float32
    )


def body(features, gate_weight, up_weight, down_weight, cotangent):
    hidden_cols = gate_weight.shape[1]
    both_weights = jnp.concatenate([gate_weight, up_weight], axis=1)
    gathered = lax.all_gather(features, "col", axis=0, tiled=True)
    cot_all = lax.all_gather(cotangent, "col", axis=0, tiled=True)
    block = gathered
    pre_acts = lax.psum_scatter(
        jnp.dot(block, both_weights, preferred_element_type=jnp.float32),
        "row",
        scatter_dimension=0,
        tiled=True,
    )
    block = cot_all
    hid_grad = lax.psum_scatter(
        times_transposed(block, down_weight), "row", scatter_dimension=0, tiled=True
    )
    gate_pre = pre_acts[:, :hidden_cols]
    up_pre = pre_acts[:, hidden_cols:]
    sig = jax.nn.sigmoid(gate_pre)
    silu_gate = gate_pre * sig
    hidden = (silu_gate * up_pre).astype(jnp.bfloat16)
    gate_grad = (hid_grad * up_pre * sig * (1.0 + gate_pre * (1.0 - sig))).astype(jnp.bfloat16)
    up_grad = (hid_grad * silu_gate).astype(jnp.bfloat16)
    hidden_all = lax.all_gather(hidden, "row", axis=0, tiled=True)
    block = hidden_all
    output = lax.psum_scatter(
        jnp.dot(block, down_weight, preferred_element_type=jnp.float32),
        "col",
        scatter_dimension=0,
        tiled=True,
    )
    gate_all, up_all = (
        lax.all_gather(gate_grad, "row", axis=0, tiled=True),
        lax.all_gather(up_grad, "row", axis=0, tiled=True),
    )
    input_grad = lax.psum_scatter(
        times_transposed(gate_all, gate_weight) + times_transposed(up_all, up_weight),
        "col",
        scatter_dimension=0,
        tiled=True,
    )
    gate_wgrad = over_tokens(gathered, gate_all)
    up_wgrad = over_tokens(gathered, up_all)
    down_wgrad = over_tokens(hidden_all, cot_all)
    return (output, input_grad, gate_wgrad, up_wgrad, down_wgrad)


def solution(mesh):
    in_specs = (P("col", "row"), P("row", "col"), P("row", "col"), P("col", "row"), P("col", "row"))
    out_specs = (
        P("col", "row"),
        P("col", "row"),
        P("row", "col"),
        P("row", "col"),
        P("col", "row"),
    )
    return jax.shard_map(body, mesh=mesh, in_specs=in_specs, out_specs=out_specs, check_vma=False)
```

profile of v0, /device:TPU:4, one launch (start us, length us, event | category | flops | bytes accessed | tf_op | source)
XLA Modules:
  0.0 628.1 jit_solution(1231802147683455028)
XLA Ops:
  7.2 0.0 reduce-scatter.15.cloned.1.call-start
  7.2 23.7 %all_gather.17 = bf16[768,512]{1,0:T(8,128)(2,1)S(1)} all-gather(bf16[48,512]{1,0:T(8,128)(2,1)} %param.9), channel_id=1, replica_groups=mesh['row'=16,'col'=16] {'col'}, dimensions={0}, use_global_device_ids=true | all-gather | bytes 835584 | tf_op jit(solution)/shard_map/all_gather | solution.py:23
  30.9 2.7 fusion.6
  33.6 0.0 reduce-scatter.13.cloned.1.call-start
  33.7 0.7 copy-done.3
  34.4 24.2 %all_gather.15 = bf16[768,512]{1,0:T(8,128)(2,1)S(1)} all-gather(bf16[48,512]{1,0:T(8,128)(2,1)S(1)} %copy-done.3), channel_id=1, replica_groups=mesh['row'=16,'col'=16] {'col'}, dimensions={0}, use_global_device_ids=true | all-gather | bytes 835584 | tf_op jit(solution)/shard_map/all_gather | solution.py:22
  58.6 0.9 copy-done.2
  59.5 5.3 convolution_bitcast_fusion
  64.7 6.1 copy.27
  70.9 0.0 all-gather.6.cloned.1.call-start
  71.0 47.9 %reduce-scatter.15.cloned.1.call-done = f32[48,896]{1,0:T(8,128)} async-done(((f32[768,896]{1,0:T(8,128)}), f32[48,896]{1,0:T(8,128)}) %reduce-scatter.15.cloned.1.call-update) | async-done | bytes 172048 | tf_op jit(solution)/shard_map/reduce_scatter | solution.py:32
  118.8 125.4 %reduce-scatter.13.cloned.1.call-done = f32[48,1792]{1,0:T(8,128)} async-done(((f32[768,1792]{1,0:T(8,128)}), f32[48,1792]{1,0:T(8,128)}) %reduce-scatter.13.cloned.1.call-update) | async-done | bytes 344080 | tf_op jit(solution)/shard_map/reduce_scatter | solution.py:25
  244.2 1.9 multiply_convert_fusion
  246.1 0.0 all-gather.8.cloned.1.call-start
  246.2 0.5 all-gather.8.cloned.1.call-update
  246.7 0.0 all-gather.4.cloned.1.call-start
  246.7 0.5 all-gather.4.cloned.1.call-update
  247.3 0.0 reduce-scatter.11.cloned.1.call-start
  247.3 69.0 %all-gather.6.cloned.1.call-done = bf16[768,896]{1,0:T(8,128)(2,1)} async-done(((bf16[48,896]{1,0:T(8,128)(2,1)}), bf16[768,896]{1,0:T(8,128)(2,1)}) %all-gather.6.cloned.1.call-update) | async-done | bytes 1376272 | tf_op jit(solution)/shard_map/all_gather | solution.py:51
  316.4 2.6 fusion.7
  319.0 69.6 %all-gather.8.cloned.1.call-done = bf16[768,896]{1,0:T(8,128)(2,1)} async-done(((bf16[48,896]{1,0:T(8,128)(2,1)}), bf16[768,896]{1,0:T(8,128)(2,1)}) %all-gather.8.cloned.1.call-update) | async-done | bytes 1376272 | tf_op jit(solution)/shard_map/all_gather | solution.py:52
  388.6 3.7 convolution_add_fusion
  392.4 0.0 reduce-scatter.9.cloned.1.call-start
  392.4 68.4 %all-gather.4.cloned.1.call-done = bf16[768,896]{1,0:T(8,128)(2,1)} async-done(((bf16[48,896]{1,0:T(8,128)(2,1)}), bf16[768,896]{1,0:T(8,128)(2,1)}) %all-gather.4.cloned.1.call-update) | async-done | bytes 1376272 | tf_op jit(solution)/shard_map/all_gather | solution.py:42
  460.8 3.5 fusion.5
  464.3 2.5 convolution_bitcast_fusion.2
  466.8 1.7 copy.24
  468.5 2.5 convolution_bitcast_fusion.1
  470.9 1.7 copy.25
  472.6 3.5 fusion.8
  476.1 64.8 %reduce-scatter.11.cloned.1.call-done = f32[48,512]{1,0:T(8,128)} async-done(((f32[768,512]{1,0:T(8,128)}), f32[48,512]{1,0:T(8,128)}) %reduce-scatter.11.cloned.1.call-update) | async-done | bytes 98320 | tf_op jit(solution)/shard_map/reduce_scatter | solution.py:54
  540.9 80.4 %reduce-scatter.9.cloned.1.call-done = f32[48,512]{1,0:T(8,128)} async-done(((f32[768,512]{1,0:T(8,128)}), f32[48,512]{1,0:T(8,128)}) %reduce-scatter.9.cloned.1.call-update) | async-done | bytes 98320 | tf_op jit(solution)/shard_map/reduce_scatter | solution.py:44
  (11 shorter events, 0.1 us)
Async XLA Ops:
  7.2 23.8 %copy-start = (bf16[896,512]{1,0:T(8,128)(2,1)S(1)}, bf16[896,512]{1,0:T(8,128)(2,1)}, u32[]{:S(2)}) copy-start(bf16[896,512]{1,0:T(8,128)(2,1)} %param.8) | copy-start | bytes 2752516
  7.2 111.7 %reduce-scatter.15.cloned.1.call-start = ((), (), s32[]{:S(2)}) async-start(), calls=%async_computation.10 | async-start | bytes 2924544 | tf_op jit(solution)/shard_map/reduce_scatter | solution.py:32
  33.6 0.8 copy-start.3
  33.6 25.8 %copy-start.1 = (bf16[512,896]{1,0:T(8,128)(2,1)S(1)}, bf16[512,896]{1,0:T(8,128)(2,1)}, u32[]{:S(2)}) copy-start(bf16[512,896]{1,0:T(8,128)(2,1)} %param.7) | copy-start | bytes 2752516
  33.6 210.6 %reduce-scatter.13.cloned.1.call-start = ((), (), s32[]{:S(2)}) async-start(), calls=%async_computation.9 | async-start | bytes 5849088 | tf_op jit(solution)/shard_map/reduce_scatter | solution.py:25
  58.6 0.9 copy-start.2
  70.9 245.5 %all-gather.6.cloned.1.call-start = ((), (), s32[]{:S(2)}) async-start(), calls=%async_computation.6 | async-start | bytes 1462272 | tf_op jit(solution)/shard_map/all_gather | solution.py:51
  246.1 142.5 %all-gather.8.cloned.1.call-start = ((), (), s32[]{:S(2)}) async-start(), calls=%async_computation.7 | async-start | bytes 1462272 | tf_op jit(solution)/shard_map/all_gather | solution.py:52
  246.7 214.2 %all-gather.4.cloned.1.call-start = ((), (), s32[]{:S(2)}) async-start(), calls=%async_computation.4 | async-start | bytes 1462272 | tf_op jit(solution)/shard_map/all_gather | solution.py:42
  247.3 293.6 %reduce-scatter.11.cloned.1.call-start = ((), (), s32[]{:S(2)}) async-start(), calls=%async_computation.8 | async-start | bytes 1671168 | tf_op jit(solution)/shard_map/reduce_scatter | solution.py:54
  392.4 228.9 %reduce-scatter.9.cloned.1.call-start = ((), (), s32[]{:S(2)}) async-start(), calls=%async_computation.5 | async-start | bytes 1671168 | tf_op jit(solution)/shard_map/reduce_scatter | solution.py:44
Sparse Core Ops, SparseCore 0:
  33.8 85.0 reduce-scatter.14
  121.6 122.6 reduce-scatter.12
  246.6 69.7 all-gather.5
  318.6 69.9 all-gather.7
  390.8 69.9 all-gather.3
  465.4 75.4 reduce-scatter.10
  545.7 75.5 reduce-scatter.8
where the time goes:
time: 630 us; the launch traced here: 628 us
  waiting for transfers between devices  527 us (84%)
  blocking collectives  47.9 us (8%)
  matrix products  26.2 us (4%)
  between operations  14.2 us (2%)
  local copies, waits for them, and re-layouts  11.1 us (2%)
    reduce_scatter x1, waiting for transfers between devices, body(): lax.psum_scatter(jnp.dot(block, both_weights, preferred_element_type=jnp....  125 us
    reduce_scatter x1, waiting for transfers between devices, body(): lax.psum_scatter(jnp.dot(block, down_weight, preferred_element_type=jnp.f...  80.4 us
    all_gather x1, waiting for transfers between devices, body(): lax.all_gather(up_grad, 'row', axis=0, tiled=True)  69.6 us
    all_gather x1, waiting for transfers between devices, body(): lax.all_gather(gate_grad, 'row', axis=0, tiled=True)  69 us
    all_gather x1, waiting for transfers between devices, body(): hidden_all = lax.all_gather(hidden, 'row', axis=0, tiled=True)  68.4 us
    reduce_scatter x1, waiting for transfers between devices, body(): lax.psum_scatter(times_transposed(gate_all, gate_weight) + times_transpos...  64.8 us
    reduce_scatter x1, waiting for transfers between devices, body(): lax.psum_scatter(times_transposed(block, down_weight), 'row', scatter_dim...  47.9 us
    all_gather x1, blocking collectives, body(): gathered = lax.all_gather(features, 'col', axis=0, tiled=True)  24.2 us
  transfers between devices with their start and end apart: 7, of which 7 were waited for; matrix products, arithmetic and copies ran while one was open for 5% of the time, Pallas kernels for 0%

commit v1 on v0

v1 whole, which is shorter than its diff:
```python
import jax
import jax.numpy as jnp
from jax import lax
from jax.experimental import pallas as pl
from jax.experimental.pallas import tpu as pltpu
from jax.sharding import PartitionSpec as P

MESH = pl.DeviceIdType.MESH
F32, BF16 = jnp.float32, jnp.bfloat16
NZ = 8
T = 48
D = 512
FA, FB = 512, 384
F = FA + FB
CA, CB = 3 * FA, 3 * FB
HALF = CA // 2
SCALE = 4096.0
CSCALE = 1024.0
ORDER = (4, 3, 5, 2, 6, 1, 7, 0)
POS = {off: at for at, off in enumerate(ORDER)}
BACK = (0, 1, 7, 2, 6, 3, 5, 4)
BPOS = {off: at for at, off in enumerate(BACK)}


def enc5(value):
    value = value * SCALE
    square = value * value
    return (square * square * value).astype(BF16)


def dec5(code):
    code = code.astype(F32)
    root = jnp.exp2(jnp.log2(jnp.abs(code)) * 0.2) * (1.0 / SCALE)
    return jnp.where(code < 0, -root, root)


def enc3(value):
    value = value * CSCALE
    return (value * value * value).astype(BF16)


def dec3(code):
    code = code.astype(F32)
    root = jnp.exp2(jnp.log2(jnp.abs(code)) * (1.0 / 3.0)) * (1.0 / CSCALE)
    return jnp.where(code < 0, -root, root)


def dot(left, right):
    return jnp.dot(left, right, preferred_element_type=F32)


def dot_t(left, right):
    return lax.dot_general(left, right, (((1,), (1,)), ((), ())), preferred_element_type=F32)


def rows(count, step=16):
    def run(fn):
        @pl.loop(0, count // step)
        def _(i):
            fn(pl.ds(pl.multiple_of(i * step, step), step))

    return run


def layer_kernel(
    x_hbm, g_hbm, u_hbm, d_hbm, c_hbm,
    out_ref, ing_ref, xc_hbm, ga_hbm, gb_hbm,
    g_w, u_w, d_w, xc, pa, pb, ya_s, ya_r, yb_s, yb_r, za_s, za_r, zb_s, zb_r,
    ga, gb, oi, sib_r, col_s, col_r,
    load_sem, ag_ss, ag_rs, fw_ss, fw_rs, ya_ss, ya_rs, yb_ss, yb_rs,
    za_ss, za_rs, zb_ss, zb_rs, gaz_ss, gaz_rs, gay_ss, gay_rs, gbz_ss, gbz_rs, gby_ss, gby_rs,
    sib_ss, sib_rs, col_ss, col_rs, store_sem,
):
    row, col = lax.axis_index("row"), lax.axis_index("col")
    z, yl = row // 2, row % 2
    chip, core = col // 2, col % 2
    x, yh = chip // 2, chip % 2

    def at_chip(k):
        return ((x + k // 2) % 4) * 2 + (yh + k % 2) % 2

    def from_chip(k):
        return ((x + 4 - k // 2) % 4) * 2 + (yh + k % 2) % 2

    up_z = ((z + 1) % NZ) * 2 + yl
    down_z = ((z + NZ - 1) % NZ) * 2 + yl
    mate = (z * 2 + 1 - yl, col)
    sibling = (row, chip * 2 + 1 - core)
    ring = ((up_z, col), (down_z, col))

    def send(src, dst, ss, rs, to):
        copy = pltpu.make_async_remote_copy(
            src_ref=src, dst_ref=dst, send_sem=ss, recv_sem=rs, device_id=to, device_id_type=MESH
        )
        copy.start()
        return copy

    sent = []

    loads = [
        pltpu.make_async_copy(x_hbm, xc.at[col, 0], load_sem.at[0]),
        pltpu.make_async_copy(c_hbm, xc.at[col, 1], load_sem.at[1]),
        pltpu.make_async_copy(g_hbm, g_w, load_sem.at[2]),
        pltpu.make_async_copy(u_hbm, u_w, load_sem.at[3]),
        pltpu.make_async_copy(d_hbm, d_w, load_sem.at[4]),
    ]
    for copy in loads:
        copy.start()

    barrier = pltpu.get_barrier_semaphore()
    for k in range(1, 8):
        pl.semaphore_signal(barrier, inc=1, device_id=(row, from_chip(k) * 2 + core), device_id_type=MESH)
    for to in (sibling, mate, ring[0], ring[1]):
        pl.semaphore_signal(barrier, inc=1, device_id=to, device_id_type=MESH)
    pl.semaphore_wait(barrier, 11)
    loads[0].wait()
    loads[1].wait()

    direct = []
    for k in (4, 5, 2, 6, 3, 7, 1):
        direct.append((k, send(xc.at[col], xc.at[col], ag_ss.at[k], ag_rs.at[k], (row, at_chip(k) * 2 + core))))
    forwarded = [send(xc.at[col], xc.at[col], fw_ss.at[0], fw_rs.at[0], sibling)]
    for k in (1, 2, 6, 3, 7, 4, 5):
        src = from_chip(k) * 2 + core
        pltpu.make_async_remote_copy(
            src_ref=xc.at[src], dst_ref=xc.at[src], send_sem=ag_ss.at[k], recv_sem=ag_rs.at[k],
            device_id=mate, device_id_type=MESH,
        ).wait_recv()
        forwarded.append(send(xc.at[src], xc.at[src], fw_ss.at[k], fw_rs.at[k], sibling))
    for copy in loads[2:]:
        copy.wait()
    for k, copy in enumerate(forwarded):
        copy.wait_recv()
    sent += [copy for _, copy in direct] + forwarded
    keep_xc = pltpu.make_async_copy(xc, xc_hbm, store_sem.at[0])
    keep_xc.start()

    def partial(at, off):
        piece = (z + off) % NZ

        def tokens(which):
            both = jnp.concatenate([xc[2 * piece + yl, which], xc[2 * piece + 1 - yl, which]], axis=0)
            return both

        feats, cots = tokens(0), tokens(1)
        pa[at, :, 0:FA] = dot(feats, g_w[:, 0:FA])
        pa[at, :, FA : 2 * FA] = dot(feats, u_w[:, 0:FA])
        pa[at, :, 2 * FA : CA] = dot_t(cots, d_w[0:FA, :])
        pb[at, :, 0:FB] = dot(feats, g_w[:, FA:F])
        pb[at, :, FB : 2 * FB] = dot(feats, u_w[:, FA:F])
        pb[at, :, 2 * FB : CB] = dot_t(cots, d_w[FA:F, :])

        @rows(T)
        def _(r):
            ya_s[at, r] = enc5(pa[at, pl.ds(pl.multiple_of(r.start + T, 16), 16)])

    def ya_send(at):
        return send(ya_s.at[at], ya_r.at[at], ya_ss.at[at], ya_rs.at[at], mate)

    def ya_wait(at):
        copy = pltpu.make_async_remote_copy(
            src_ref=ya_s.at[at], dst_ref=ya_r.at[at], send_sem=ya_ss.at[at], recv_sem=ya_rs.at[at],
            device_id=mate, device_id_type=MESH,
        )
        copy.wait_recv()
        return copy

    def za_part(way, step):
        if step:
            return (way, step)
        return (way, step, slice(None), pl.ds(way * HALF, HALF))

    def zb_part(way, step):
        if step:
            return (way, step)
        return (way, step, pl.ds(way * T, T))

    def za_send(way, step):
        part = za_part(way, step)
        copy = send(za_s.at[part], za_r.at[part], za_ss.at[way, step], za_rs.at[way, step], ring[way])
        sent.append(copy)
        return copy

    def zb_send(way, step):
        part = zb_part(way, step)
        copy = send(zb_s.at[part], zb_r.at[part], zb_ss.at[way, step], zb_rs.at[way, step], ring[way])
        sent.append(copy)
        return copy

    partial(0, 4)
    ya_send(0)
    for way in range(2):
        @rows(T)
        def _(r, way=way):
            zb_s[way, 0, pl.ds(pl.multiple_of(r.start + way * T, 16), 16)] = enc5(
                pb[0, pl.ds(pl.multiple_of(r.start + way * T, 16), 16)]
            )

    zb_moves = {(way, 0): zb_send(way, 0) for way in range(2)}

    @pl.loop(1, NZ)
    def _(at):
        off = jnp.where(at % 2 == 1, 4 - (at + 1) // 2, 4 + at // 2)
        partial(at, off)
        ya_send(at)

    ya_wait(0)
    for way in range(2):
        cols = pl.ds(way * HALF, HALF)

        @rows(T)
        def _(r, cols=cols, way=way):
            za_s[way, 0, r, cols] = enc5(pa[0, r, cols] + dec5(ya_r[0, r, cols]))

    za_moves = {(way, 0): za_send(way, 0) for way in range(2)}

    for step in range(1, 4):
        for way in range(2):
            at = POS[4 - step if way == 0 else 4 + step]
            zb_moves[way, step - 1].wait_recv()
            if step == 1:
                got = way * T

                @rows(T)
                def _(r, got=got, at=at, way=way):
                    r1 = pl.ds(pl.multiple_of(r.start + got, 16), 16)
                    zb_s[way, 1, r1] = enc5(pb[at, r1] + dec5(zb_r[way, 0, r1]))
                    r2 = pl.ds(pl.multiple_of(r.start + (T - got), 16), 16)
                    zb_s[way, 1, r2] = enc5(pb[at, r2])
            else:

                @rows(2 * T)
                def _(r, at=at, way=way, step=step):
                    zb_s[way, step, r] = enc5(pb[at, r] + dec5(zb_r[way, step - 1, r]))

            zb_moves[way, step] = zb_send(way, step)
        for way in range(2):
            at = POS[4 - step if way == 0 else 4 + step]
            ya_wait(at)
            za_moves[way, step - 1].wait_recv()
            if step == 1:
                got = pl.ds(way * HALF, HALF)
                rest = pl.ds((1 - way) * HALF, HALF)

                @rows(T)
                def _(r, got=got, rest=rest, at=at, way=way):
                    za_s[way, 1, r, got] = enc5(
                        pa[at, r, got] + dec5(ya_r[at, r, got]) + dec5(za_r[way, 0, r, got])
                    )
                    za_s[way, 1, r, rest] = enc5(pa[at, r, rest] + dec5(ya_r[at, r, rest]))
            else:

                @rows(T)
                def _(r, at=at, way=way, step=step):
                    za_s[way, step, r] = enc5(
                        pa[at, r] + dec5(ya_r[at, r]) + dec5(za_r[way, step - 1, r])
                    )

            za_moves[way, step] = za_send(way, step)

    for way in range(2):
        zb_moves[way, 3].wait_recv()

    @rows(T)
    def _(r):
        r2 = pl.ds(pl.multiple_of(r.start + T, 16), 16)
        yb_s[r] = enc5(pb[7, r2] + dec5(zb_r[0, 3, r2]) + dec5(zb_r[1, 3, r2]))

    yb_move = send(yb_s, yb_r, yb_ss, yb_rs, mate)
    sent.append(yb_move)

    def activate(gate, up, hid):
        sig = jax.nn.sigmoid(gate)
        silu = gate * sig
        return (
            (silu * up).astype(BF16),
            (hid * up * sig * (1.0 + gate * (1.0 - sig))).astype(BF16),
            (hid * silu).astype(BF16),
        )

    ya_wait(7)
    for way in range(2):
        za_moves[way, 3].wait_recv()

    @rows(T)
    def _(r):
        def total(first):
            cols = pl.ds(first, FA)
            return pa[7, r, cols] + dec5(ya_r[7, r, cols]) + dec5(za_r[0, 3, r, cols]) + dec5(za_r[1, 3, r, cols])

        hidden, gate_grad, up_grad = activate(total(0), total(FA), total(2 * FA))
        ga[row, r, 0:FA] = hidden
        ga[row, r, FA : 2 * FA] = gate_grad
        ga[row, r, 2 * FA : CA] = up_grad

    def gaz_send(way, step):
        src = ((z + NZ - step) % NZ if way == 0 else (z + step) % NZ) * 2 + yl
        if step < 3:
            part = ga.at[src]
        else:
            part = ga.at[src, :, pl.ds(way * HALF, HALF)]
        copy = send(part, part, gaz_ss.at[way, step], gaz_rs.at[way, step], ring[way])
        sent.append(copy)

    def gaz_wait(way, step):
        src = ((z + NZ - 1 - step) % NZ if way == 0 else (z + step + 1) % NZ) * 2 + yl
        if step < 3:
            part = ga.at[src]
        else:
            part = ga.at[src, :, pl.ds(way * HALF, HALF)]
        pltpu.make_async_remote_copy(
            src_ref=part, dst_ref=part, send_sem=gaz_ss.at[way, step], recv_sem=gaz_rs.at[way, step],
            device_id=mate, device_id_type=MESH,
        ).wait_recv()

    def gay_send(off):
        part = ga.at[((z + off) % NZ) * 2 + yl]
        sent.append(send(part, part, gay_ss.at[off], gay_rs.at[off], mate))

    def gay_wait(off):
        part = ga.at[((z + off) % NZ) * 2 + 1 - yl]
        pltpu.make_async_remote_copy(
            src_ref=part, dst_ref=part, send_sem=gay_ss.at[off], recv_sem=gay_rs.at[off],
            device_id=mate, device_id_type=MESH,
        ).wait_recv()

    def gbz_part(way, step, src):
        if step < 3:
            return gb.at[pl.ds(2 * src, 2)]
        return gb.at[2 * src + way]

    def gbz_send(way, step):
        part = gbz_part(way, step, (z + NZ - step) % NZ if way == 0 else (z + step) % NZ)
        sent.append(send(part, part, gbz_ss.at[way, step], gbz_rs.at[way, step], ring[way]))

    def gbz_wait(way, step):
        part = gbz_part(way, step, (z + NZ - 1 - step) % NZ if way == 0 else (z + step + 1) % NZ)
        pltpu.make_async_remote_copy(
            src_ref=part, dst_ref=part, send_sem=gbz_ss.at[way, step], recv_sem=gbz_rs.at[way, step],
            device_id=mate, device_id_type=MESH,
        ).wait_recv()

    for way in range(2):
        gaz_send(way, 0)
    yb_move.wait_recv()

    @rows(T)
    def _(r):
        def total(first):
            cols = pl.ds(first, FB)
            return (
                pb[7, r, cols] + dec5(zb_r[0, 3, r, cols]) + dec5(zb_r[1, 3, r, cols]) + dec5(yb_r[r, cols])
            )

        hidden, gate_grad, up_grad = activate(total(0), total(FB), total(2 * FB))
        gb[row, r, 0:FB] = hidden
        gb[row, r, FB : 2 * FB] = gate_grad
        gb[row, r, 2 * FB : CB] = up_grad

    part = gb.at[row]
    sent.append(send(part, part, gby_ss, gby_rs, mate))
    gay_send(0)

    def products(at, off):
        piece = (z + off) % NZ
        both = pl.ds(2 * piece, 2)

        def part(ref, first, width):
            return ref[both, :, first : first + width].reshape(2 * T, width)

        outs = dot(part(ga, 0, FA), d_w[0:FA, :]) + dot(part(gb, 0, FB), d_w[FA:F, :])
        grads = (
            dot_t(part(ga, FA, FA), g_w[:, 0:FA])
            + dot_t(part(ga, 2 * FA, FA), u_w[:, 0:FA])
            + dot_t(part(gb, FB, FB), g_w[:, FA:F])
            + dot_t(part(gb, 2 * FB, FB), u_w[:, FA:F])
        )
        oi[at, :, :, 0:D] = outs.reshape(2, T, D)
        oi[at, :, :, D : 2 * D] = grads.reshape(2, T, D)
        send(oi.at[at, 1 - core], sib_r.at[at], sib_ss.at[at], sib_rs.at[at], sibling)

    def sib_copy(at):
        return pltpu.make_async_remote_copy(
            src_ref=oi.at[at, 1 - core], dst_ref=sib_r.at[at], send_sem=sib_ss.at[at], recv_sem=sib_rs.at[at],
            device_id=sibling, device_id_type=MESH,
        )

    def col_copy(at, k, to):
        return pltpu.make_async_remote_copy(
            src_ref=col_s.at[at], dst_ref=col_r.at[k], send_sem=col_ss.at[k], recv_sem=col_rs.at[k],
            device_id=(row, to * 2 + core), device_id_type=MESH,
        )

    def reduce_to_owner(at, off):
        piece = (z + off) % NZ
        sib_copy(at).wait_recv()

        @pl.when(piece == chip)
        def _():
            out_ref[...] = oi[at, core, :, 0:D] + sib_r[at, :, 0:D]
            ing_ref[...] = oi[at, core, :, D : 2 * D] + sib_r[at, :, D : 2 * D]

        @pl.when(piece != chip)
        def _():
            @rows(T)
            def _(r):
                col_s[at, r] = enc3(oi[at, core, r] + sib_r[at, r])

            k = ((piece // 2 + 4 - x) % 4) * 2 + (piece + yh) % 2
            col_copy(at, k, piece).start()

    gby = gb.at[mate[0]]
    pltpu.make_async_remote_copy(
        src_ref=gby, dst_ref=gby, send_sem=gby_ss, recv_sem=gby_rs, device_id=mate, device_id_type=MESH
    ).wait_recv()
    for way in range(2):
        gbz_send(way, 0)

    def offs_of(step):
        return (NZ - 1 - step, step + 1)

    for step in range(4):
        for way in range(2):
            gaz_wait(way, step)
            if step < 3:
                gaz_send(way, step + 1)
                gay_send(offs_of(step)[way])
        if step == 3:
            gay_send(4)
        if step == 0:
            gay_wait(0)
            products(0, 0)
        else:
            for way in range(2):
                off = offs_of(step - 1)[way]
                gay_wait(off)
                products(BPOS[off], off)
        for way in range(2):
            gbz_wait(way, step)
            if step < 3:
                gbz_send(way, step + 1)
        if step == 0:
            reduce_to_owner(0, 0)
        else:
            for way in range(2):
                off = offs_of(step - 1)[way]
                reduce_to_owner(BPOS[off], off)

    gay_wait(4)
    products(7, 4)
    keep_ga = pltpu.make_async_copy(ga, ga_hbm, store_sem.at[1])
    keep_gb = pltpu.make_async_copy(gb, gb_hbm, store_sem.at[2])
    keep_ga.start()
    keep_gb.start()
    reduce_to_owner(7, 4)
    for k in range(1, 8):
        col_copy(0, k, at_chip(k)).wait_recv()

        @rows(T)
        def _(r, k=k):
            out_ref[r] += dec3(col_r[k, r, 0:D])
            ing_ref[r] += dec3(col_r[k, r, D : 2 * D])

    for copy in sent:
        copy.wait_send()

    @pl.loop(0, NZ)
    def _(at):
        pltpu.make_async_remote_copy(
            src_ref=ya_s.at[at], dst_ref=ya_r.at[at], send_sem=ya_ss.at[at], recv_sem=ya_rs.at[at],
            device_id=mate, device_id_type=MESH,
        ).wait_send()
        sib_copy(at).wait_send()

    for k in range(1, 8):
        col_copy(0, k, at_chip(k)).wait_send()
    keep_xc.wait()
    keep_ga.wait()
    keep_gb.wait()


def layer(features, gate_weight, up_weight, down_weight, cotangent):
    vmem = pltpu.VMEM
    dma = pltpu.SemaphoreType.DMA
    hbm = pl.BlockSpec(memory_space=pl.ANY)
    full = pl.BlockSpec(memory_space=pltpu.VMEM)
    return pl.pallas_call(
        layer_kernel,
        out_shape=(
            jax.ShapeDtypeStruct((T, D), F32),
            jax.ShapeDtypeStruct((T, D), F32),
            jax.ShapeDtypeStruct((16, 2, T, D), BF16),
            jax.ShapeDtypeStruct((16, T, CA), BF16),
            jax.ShapeDtypeStruct((16, T, CB), BF16),
        ),
        in_specs=[hbm] * 5,
        out_specs=(full, full, hbm, hbm, hbm),
        scratch_shapes=[
            vmem((D, F), BF16),
            vmem((D, F), BF16),
            vmem((F, D), BF16),
            vmem((16, 2, T, D), BF16),
            vmem((NZ, 2 * T, CA), F32),
            vmem((NZ, 2 * T, CB), F32),
            vmem((NZ, T, CA), BF16),
            vmem((NZ, T, CA), BF16),
            vmem((T, CB), BF16),
            vmem((T, CB), BF16),
            vmem((2, 4, T, CA), BF16),
            vmem((2, 4, T, CA), BF16),
            vmem((2, 4, 2 * T, CB), BF16),
            vmem((2, 4, 2 * T, CB), BF16),
            vmem((16, T, CA), BF16),
            vmem((16, T, CB), BF16),
            vmem((NZ, 2, T, 2 * D), F32),
            vmem((NZ, T, 2 * D), F32),
            vmem((NZ, T, 2 * D), BF16),
            vmem((NZ, T, 2 * D), BF16),
            dma((5,)),
            dma((8,)), dma((8,)), dma((8,)), dma((8,)),
            dma((8,)), dma((8,)), dma, dma,
            dma((2, 4)), dma((2, 4)), dma((2, 4)), dma((2, 4)),
            dma((2, 4)), dma((2, 4)), dma((8,)), dma((8,)),
            dma((2, 4)), dma((2, 4)), dma, dma,
            dma((8,)), dma((8,)), dma((8,)), dma((8,)),
            dma((3,)),
        ],
        compiler_params=pltpu.CompilerParams(
            collective_id=0, has_side_effects=True, vmem_limit_bytes=50 * 1024 * 1024
        ),
        name="layer",
    )(features, gate_weight, up_weight, down_weight, cotangent)


def wgrad_kernel(xc_ref, ga_ref, gb_ref, g_out, u_out, d_out):
    tokens = 16 * T
    over = (((0,), (0,)), ((), ()))

    def product(left, right):
        return lax.dot_general(left, right, over, preferred_element_type=F32)

    feats = xc_ref[:, 0].reshape(tokens, D)
    cots = xc_ref[:, 1].reshape(tokens, D)
    for ref, width, first in ((ga_ref, FA, 0), (gb_ref, FB, FA)):
        hidden = ref[:, :, 0:width].reshape(tokens, width)
        d_out[first : first + width, :] = product(hidden, cots)
        g_out[:, first : first + width] = product(feats, ref[:, :, width : 2 * width].reshape(tokens, width))
        u_out[:, first : first + width] = product(feats, ref[:, :, 2 * width : 3 * width].reshape(tokens, width))


def wgrads(xc, ga, gb):
    return pl.pallas_call(
        wgrad_kernel,
        out_shape=(
            jax.ShapeDtypeStruct((D, F), F32),
            jax.ShapeDtypeStruct((D, F), F32),
            jax.ShapeDtypeStruct((F, D), F32),
        ),
        compiler_params=pltpu.CompilerParams(vmem_limit_bytes=50 * 1024 * 1024),
        name="wgrads",
    )(xc, ga, gb)


def body(features, gate_weight, up_weight, down_weight, cotangent):
    output, input_grad, xc, ga, gb = layer(features, gate_weight, up_weight, down_weight, cotangent)
    gate_wgrad, up_wgrad, down_wgrad = wgrads(xc, ga, gb)
    return (output, input_grad, gate_wgrad, up_wgrad, down_wgrad)


def solution(mesh):
    in_specs = (P("col", "row"), P("row", "col"), P("row", "col"), P("col", "row"), P("col", "row"))
    out_specs = (
        P("col", "row"),
        P("col", "row"),
        P("row", "col"),
        P("row", "col"),
        P("col", "row"),
    )
    return jax.shard_map(body, mesh=mesh, in_specs=in_specs, out_specs=out_specs, check_vma=False)
```

time: 630 us -> 128 us (0.20)
  waiting for transfers between devices: 527 us -> 0 us
  Pallas kernels: 0 us -> 118 us
  blocking collectives: 47.9 us -> 0 us
  matrix products: 26.2 us -> 0 us
  between operations: 14.2 us -> 0.66 us
    reduce_scatter x4 -> x0, waiting for transfers between devices: 318 us -> none  [the longest x1 125 us: body(): lax.psum_scatter(jnp.dot(block, both_weights, preferred_element_type=jnp....]
    all_gather x3 -> x0, waiting for transfers between devices: 207 us -> none  [the longest x1 69.6 us: body(): lax.all_gather(up_grad, 'row', axis=0, tiled=True)]
    pallas_call x0 -> x2, Pallas kernels: none -> 118 us  [the longest x1 111 us: layer(): pl.pallas_call(layer_kernel, out_shape=(jax.ShapeDtypeStruct((T, D), F32)...]
    all_gather x2 -> x0, blocking collectives: 47.9 us -> none  [the longest x1 24.2 us: body(): gathered = lax.all_gather(features, 'col', axis=0, tiled=True)]
    dot_general x7 -> x0, matrix products: 23.5 us -> none  [the longest x3 8.38 us: over_tokens(): lax.dot_general(left, right, (((0,), (0,)), ((), ())), preferred_element_...]
  transfers between devices with their start and end apart: 7 -> 0, of which waited for: 7 -> 0; matrix products, arithmetic and copies ran while one was open for 5% -> 0% of each run, Pallas kernels for 0% -> 0%
where the time goes in v1:
time: 128 us
  Pallas kernels  118 us (92%)
  local copies, waits for them, and re-layouts  9.28 us (7%)
    pallas_call x1, Pallas kernels, layer(): pl.pallas_call(layer_kernel, out_shape=(jax.ShapeDtypeStruct((T, D), F32)...  111 us
    unnamed x16, local copies, waits for them, and re-layouts  9.28 us
    pallas_call x1, Pallas kernels, wgrads(): pl.pallas_call(wgrad_kernel, out_shape=(jax.ShapeDtypeStruct((D, F), F32)...  6.26 us

profile of v1, /device:TPU:4, one launch (start us, length us, event | category | flops | bytes accessed | tf_op | source)
XLA Modules:
  0.0 127.5 jit_solution(9359939131796492594)
XLA Ops:
  0.6 0.0 copy-start.2
  0.6 1.2 copy-done.2
  1.8 0.0 copy-start.3
  1.8 1.2 copy-done.3
  3.0 0.0 copy-start.4
  3.0 1.2 copy-done.4
  4.2 0.0 copy-start.5
  4.2 0.8 copy-done.5
  5.0 0.0 copy-start.6
  5.0 0.8 copy-done.6
  5.8 111.3 %layer.1 = (f32[48,512]{1,0:T(8,128)S(1)}, f32[48,512]{1,0:T(8,128)S(1)}, bf16[16,2,48,512]{3,2,1,0:T(8,128)(2,1)}, bf16[16,48,1536]{2,1,0:T(8,128)(2,1)}, bf16[16,48,1152]{2,1,0:T(8,128)(2,1)}) custom-call(bf16[48,512]{1,0:T(8,128)(2,1)S(1)} %copy-done.5, bf16[512,896]{1,0:T(8,128)(2,1)S(1)} %copy-done.2, bf16[512,896]{1,0:T(8,128)(2,1)S(1)} %copy-done.3, ...), custom_call_target="tpu_custom_call" | custom-call | tf_op jit(solution)/shard_map/layer/pallas_call | solution.py:487
  117.1 0.0 copy-start
  117.1 1.5 %copy-done = bf16[16,48,1152]{2,1,0:T(8,128)(2,1)S(1)} copy-done((bf16[16,48,1152]{2,1,0:T(8,128)(2,1)S(1)}, bf16[16,48,1152]{2,1,0:T(8,128)(2,1)}, u32[]{:S(2)}) %copy-start) | copy-done | bytes 1769496
  118.6 0.0 copy-start.1
  118.6 1.4 %copy-done.1 = bf16[16,2,48,512]{3,2,1,0:T(8,128)(2,1)S(1)} copy-done((bf16[16,2,48,512]{3,2,1,0:T(8,128)(2,1)S(1)}, bf16[16,2,48,512]{3,2,1,0:T(8,128)(2,1)}, u32[]{:S(2)}) %copy-start.1) | copy-done | bytes 1572888
  120.0 6.3 %wgrads.1 = (f32[512,896]{1,0:T(8,128)}, f32[512,896]{1,0:T(8,128)}, f32[896,512]{1,0:T(8,128)}) custom-call(bf16[16,2,48,512]{3,2,1,0:T(8,128)(2,1)S(1)} %copy-done.1, bf16[16,48,1536]{2,1,0:T(8,128)(2,1)} %get-tuple-element.16.ga_ref, bf16[16,48,1152]{2,1,0:T(8,128)(2,1)S(1)} %copy-done), custom_call_target="tpu_custom_call" | custom-call | tf_op jit(solution)/shard_map/wgrads/pallas_call | solution.py:552
  126.2 0.6 copy.12
  126.9 0.6 copy.13
Async XLA Ops:
  0.6 1.2 copy-start.2
  1.8 1.2 copy-start.3
  3.0 1.2 copy-start.4
  4.2 0.8 copy-start.5
  5.0 0.8 copy-start.6
  117.1 1.5 %copy-start = (bf16[16,48,1152]{2,1,0:T(8,128)(2,1)S(1)}, bf16[16,48,1152]{2,1,0:T(8,128)(2,1)}, u32[]{:S(2)}) copy-start(bf16[16,48,1152]{2,1,0:T(8,128)(2,1)} %get-tuple-element.17.gb_ref) | copy-start | bytes 5308420
  118.6 1.4 %copy-start.1 = (bf16[16,2,48,512]{3,2,1,0:T(8,128)(2,1)S(1)}, bf16[16,2,48,512]{3,2,1,0:T(8,128)(2,1)}, u32[]{:S(2)}) copy-start(bf16[16,2,48,512]{3,2,1,0:T(8,128)(2,1)} %get-tuple-element.15.xc_ref) | copy-start | bytes 4718596

commit v2 on v1

--- a/solution.py
+++ b/solution.py
@@ -64,12 +64,12 @@
 
 def layer_kernel(
     x_hbm, g_hbm, u_hbm, d_hbm, c_hbm,
-    out_ref, ing_ref, xc_hbm, ga_hbm, gb_hbm,
-    g_w, u_w, d_w, xc, pa, pb, ya_s, ya_r, yb_s, yb_r, za_s, za_r, zb_s, zb_r,
-    ga, gb, oi, sib_r, col_s, col_r,
-    load_sem, ag_ss, ag_rs, fw_ss, fw_rs, ya_ss, ya_rs, yb_ss, yb_rs,
-    za_ss, za_rs, zb_ss, zb_rs, gaz_ss, gaz_rs, gay_ss, gay_rs, gbz_ss, gbz_rs, gby_ss, gby_rs,
-    sib_ss, sib_rs, col_ss, col_rs, store_sem,
+    out_ref, ing_ref, g_out, u_out, d_out,
+    g_w, u_w, d_w, xf, xc, ft, pa, pb, ya_s, ya_r, yb_s, yb_r, za_s, za_r, zb_s, zb_r,
+    ga, gb, oi, sib_r, col_s, col_r, acc, fin_s, fin_r,
+    load_sem, f_ss, f_rs, c_ss, c_rs, ff_ss, ff_rs, cf_ss, cf_rs, ya_ss, ya_rs, yb_ss, yb_rs,
+    za_ss, za_rs, zb_ss, zb_rs, zh_ss, zh_rs, gaz_ss, gaz_rs, gay_ss, gay_rs, gbz_ss, gbz_rs, gby_ss, gby_rs,
+    sib_ss, sib_rs, col_ss, col_rs, fin_ss, fin_rs,
 ):
     row, col = lax.axis_index("row"), lax.axis_index("col")
     z, yl = row // 2, row % 2
@@ -98,8 +98,8 @@
     sent = []
 
     loads = [
-        pltpu.make_async_copy(x_hbm, xc.at[col, 0], load_sem.at[0]),
-        pltpu.make_async_copy(c_hbm, xc.at[col, 1], load_sem.at[1]),
+        pltpu.make_async_copy(x_hbm, xf.at[col], load_sem.at[0]),
+        pltpu.make_async_copy(c_hbm, xc.at[col], load_sem.at[1]),
         pltpu.make_async_copy(g_hbm, g_w, load_sem.at[2]),
         pltpu.make_async_copy(u_hbm, u_w, load_sem.at[3]),
         pltpu.make_async_copy(d_hbm, d_w, load_sem.at[4]),
@@ -116,64 +116,84 @@
     loads[0].wait()
     loads[1].wait()
 
-    direct = []
+    def arrival(ref, ss, rs):
+        return pltpu.make_async_remote_copy(
+            src_ref=ref, dst_ref=ref, send_sem=ss, recv_sem=rs, device_id=mate, device_id_type=MESH
+        )
+
+    def same_core(k):
+        return (row, at_chip(k) * 2 + core)
+
+    mine_f, mine_c = xf.at[col], xc.at[col]
     for k in (4, 5, 2, 6, 3, 7, 1):
-        direct.append((k, send(xc.at[col], xc.at[col], ag_ss.at[k], ag_rs.at[k], (row, at_chip(k) * 2 + core))))
-    forwarded = [send(xc.at[col], xc.at[col], fw_ss.at[0], fw_rs.at[0], sibling)]
+        sent.append(send(mine_f, mine_f, f_ss.at[k], f_rs.at[k], same_core(k)))
+    sent.append(send(mine_f, mine_f, ff_ss.at[0], ff_rs.at[0], sibling))
+    for k in (1, 4, 2, 6):
+        sent.append(send(mine_c, mine_c, c_ss.at[k], c_rs.at[k], same_core(k)))
+    sent.append(send(mine_c, mine_c, cf_ss.at[0], cf_rs.at[0], sibling))
+
+    def pass_on(ref, ss, rs, to_ss, to_rs, k):
+        part = ref.at[from_chip(k) * 2 + core]
+        arrival(part, ss.at[k], rs.at[k]).wait_recv()
+        sent.append(send(part, part, to_ss.at[k], to_rs.at[k], sibling))
+
     for k in (1, 2, 6, 3, 7, 4, 5):
-        src = from_chip(k) * 2 + core
-        pltpu.make_async_remote_copy(
-            src_ref=xc.at[src], dst_ref=xc.at[src], send_sem=ag_ss.at[k], recv_sem=ag_rs.at[k],
-            device_id=mate, device_id_type=MESH,
-        ).wait_recv()
-        forwarded.append(send(xc.at[src], xc.at[src], fw_ss.at[k], fw_rs.at[k], sibling))
+        pass_on(xf, f_ss, f_rs, ff_ss, ff_rs, k)
+    pass_on(xc, c_ss, c_rs, cf_ss, cf_rs, 1)
+    partner = xc.at[from_chip(1) * 2 + core]
+    for k in (5, 3, 7):
+        sent.append(send(partner, partner, c_ss.at[k], c_rs.at[k], same_core(k - 1)))
     for copy in loads[2:]:
         copy.wait()
-    for k, copy in enumerate(forwarded):
-        copy.wait_recv()
-    sent += [copy for _, copy in direct] + forwarded
-    keep_xc = pltpu.make_async_copy(xc, xc_hbm, store_sem.at[0])
-    keep_xc.start()
-
-    def partial(at, off):
+    for k in range(8):
+        arrival(mine_f, ff_ss.at[k], ff_rs.at[k]).wait_recv()
+
+    def tokens(ref, off):
         piece = (z + off) % NZ
-
-        def tokens(which):
-            both = jnp.concatenate([xc[2 * piece + yl, which], xc[2 * piece + 1 - yl, which]], axis=0)
-            return both
-
-        feats, cots = tokens(0), tokens(1)
+        return jnp.concatenate([ref[2 * piece + yl], ref[2 * piece + 1 - yl]], axis=0)
+
+    def mates(r):
+        return pl.ds(pl.multiple_of(r.start + T, 16), 16)
+
+    def partial_gu(at, off):
+        feats = tokens(xf, off)
         pa[at, :, 0:FA] = dot(feats, g_w[:, 0:FA])
         pa[at, :, FA : 2 * FA] = dot(feats, u_w[:, 0:FA])
-        pa[at, :, 2 * FA : CA] = dot_t(cots, d_w[0:FA, :])
         pb[at, :, 0:FB] = dot(feats, g_w[:, FA:F])
         pb[at, :, FB : 2 * FB] = dot(feats, u_w[:, FA:F])
-        pb[at, :, 2 * FB : CB] = dot_t(cots, d_w[FA:F, :])
 
         @rows(T)
         def _(r):
-            ya_s[at, r] = enc5(pa[at, pl.ds(pl.multiple_of(r.start + T, 16), 16)])
-
-    def ya_send(at):
-        return send(ya_s.at[at], ya_r.at[at], ya_ss.at[at], ya_rs.at[at], mate)
-
-    def ya_wait(at):
-        copy = pltpu.make_async_remote_copy(
-            src_ref=ya_s.at[at], dst_ref=ya_r.at[at], send_sem=ya_ss.at[at], recv_sem=ya_rs.at[at],
+            ya_s[at, r, 0 : 2 * FA] = enc5(pa[at, mates(r), 0 : 2 * FA])
+
+    def partial_h(at, off):
+        cots = tokens(xc, off)
+        pa[at, :, 2 * FA : CA] = dot_t(cots, d_w[0:FA, :])
+        pb[at, :, 2 * FB : CB] = dot_t(cots, d_w[FA:F, :])
+
+        @rows(T)
+        def _(r):
+            ya_s[at, r, 2 * FA : CA] = enc5(pa[at, mates(r), 2 * FA : CA])
+
+    YA_COLS = (pl.ds(0, 2 * FA), pl.ds(2 * FA, FA))
+    ZB_COLS = (pl.ds(0, 2 * FB), pl.ds(2 * FB, FB))
+
+    def ya_copy(at, which):
+        cols = YA_COLS[which]
+        return pltpu.make_async_remote_copy(
+            src_ref=ya_s.at[at, :, cols], dst_ref=ya_r.at[at, :, cols],
+            send_sem=ya_ss.at[at, which], recv_sem=ya_rs.at[at, which],
             device_id=mate, device_id_type=MESH,
         )
-        copy.wait_recv()
-        return copy
+
+    def ya_wait(at):
+        for which in range(2):
+            ya_copy(at, which).wait_recv()
 
     def za_part(way, step):
         if step:
             return (way, step)
         return (way, step, slice(None), pl.ds(way * HALF, HALF))
-
-    def zb_part(way, step):
-        if step:
-            return (way, step)
-        return (way, step, pl.ds(way * T, T))
 
     def za_send(way, step):
         part = za_part(way, step)
@@ -182,27 +202,69 @@
         return copy
 
     def zb_send(way, step):
-        part = zb_part(way, step)
+        part = (way, step)
         copy = send(zb_s.at[part], zb_r.at[part], zb_ss.at[way, step], zb_rs.at[way, step], ring[way])
         sent.append(copy)
         return copy
 
-    partial(0, 4)
-    ya_send(0)
-    for way in range(2):
-        @rows(T)
-        def _(r, way=way):
-            zb_s[way, 0, pl.ds(pl.multiple_of(r.start + way * T, 16), 16)] = enc5(
-                pb[0, pl.ds(pl.multiple_of(r.start + way * T, 16), 16)]
-            )
-
-    zb_moves = {(way, 0): zb_send(way, 0) for way in range(2)}
-
-    @pl.loop(1, NZ)
+    def off_at(at):
+        return jnp.where(at % 2 == 1, 4 - (at + 1) // 2, 4 + at // 2)
+
+    zb_moves = {}
+    zh_moves = {}
+
+    def zb_first(which):
+        cols = ZB_COLS[which]
+        for way in range(2):
+            @rows(T)
+            def _(r, way=way):
+                r2 = pl.ds(pl.multiple_of(r.start + way * T, 16), 16)
+                zb_s[way, 0, r2, cols] = enc5(pb[0, r2, cols])
+
+            part = (way, 0, pl.ds(way * T, T), cols)
+            ss, rs = ((zb_ss, zb_rs), (zh_ss, zh_rs))[which]
+            at = (way, 0) if which == 0 else way
+            copy = send(zb_s.at[part], zb_r.at[part], ss.at[at], rs.at[at], ring[way])
+            sent.append(copy)
+            if which == 0:
+                zb_moves[way, 0] = copy
+            else:
+                zh_moves[way] = copy
+
+    partial_gu(0, 4)
+    ya_copy(0, 0).start()
+    zb_first(0)
+
+    @pl.loop(1, 3)
     def _(at):
-        off = jnp.where(at % 2 == 1, 4 - (at + 1) // 2, 4 + at // 2)
-        partial(at, off)
-        ya_send(at)
+        partial_gu(at, off_at(at))
+        ya_copy(at, 0).start()
+
+    for k in (2, 6, 4, 3, 7, 5):
+        pass_on(xc, c_ss, c_rs, cf_ss, cf_rs, k)
+
+    @pl.loop(3, NZ)
+    def _(at):
+        partial_gu(at, off_at(at))
+
+    for k in range(8):
+        arrival(mine_c, cf_ss.at[k], cf_rs.at[k]).wait_recv()
+    partial_h(0, 4)
+    ya_copy(0, 1).start()
+    zb_first(1)
+
+    @pl.loop(1, 3)
+    def _(at):
+        partial_h(at, off_at(at))
+        ya_copy(at, 1).start()
+
+    @pl.loop(3, NZ)
+    def _(at):
+        partial_h(at, off_at(at))
+        ya_copy(at, 0).start()
+        ya_copy(at, 1).start()
+
+    ft[...] = xf[...].reshape(16 * T, D).T
 
     ya_wait(0)
     for way in range(2):
@@ -219,6 +281,7 @@
             at = POS[4 - step if way == 0 else 4 + step]
             zb_moves[way, step - 1].wait_recv()
             if step == 1:
+                zh_moves[way].wait_recv()
                 got = way * T
 
                 @rows(T)
@@ -385,29 +448,73 @@
             device_id=sibling, device_id_type=MESH,
         )
 
-    def col_copy(at, k, to):
+    def col_copy(at, side, dist, to):
         return pltpu.make_async_remote_copy(
-            src_ref=col_s.at[at], dst_ref=col_r.at[k], send_sem=col_ss.at[k], recv_sem=col_rs.at[k],
+            src_ref=col_s.at[at], dst_ref=col_r.at[side, dist - 1],
+            send_sem=col_ss.at[side, dist - 1], recv_sem=col_rs.at[side, dist - 1],
             device_id=(row, to * 2 + core), device_id_type=MESH,
         )
 
-    def reduce_to_owner(at, off):
+    fin_move = pltpu.make_async_remote_copy(
+        src_ref=fin_s, dst_ref=fin_r, send_sem=fin_ss, recv_sem=fin_rs,
+        device_id=same_core(1), device_id_type=MESH,
+    )
+
+    def send_x(at, off):
         piece = (z + off) % NZ
+        to_x, side = piece // 2, piece % 2
         sib_copy(at).wait_recv()
 
-        @pl.when(piece == chip)
+        @pl.when(to_x == x)
         def _():
-            out_ref[...] = oi[at, core, :, 0:D] + sib_r[at, :, 0:D]
-            ing_ref[...] = oi[at, core, :, D : 2 * D] + sib_r[at, :, D : 2 * D]
-
-        @pl.when(piece != chip)
+            acc[side] = oi[at, core] + sib_r[at]
+
+        @pl.when(to_x != x)
         def _():
             @rows(T)
             def _(r):
                 col_s[at, r] = enc3(oi[at, core, r] + sib_r[at, r])
 
-            k = ((piece // 2 + 4 - x) % 4) * 2 + (piece + yh) % 2
-            col_copy(at, k, piece).start()
+            col_copy(at, side, (to_x + 4 - x) % 4, to_x * 2 + yh).start()
+
+    def reduce_x(off):
+        piece = (z + off) % NZ
+        side = piece % 2
+
+        @pl.when(piece // 2 == x)
+        def _():
+            for dist in (1, 3, 2):
+                col_copy(0, side, dist, chip).wait_recv()
+
+            @rows(T)
+            def _(r):
+                total = acc[side, r] + dec3(col_r[side, 0, r]) + dec3(col_r[side, 1, r]) + dec3(col_r[side, 2, r])
+
+                @pl.when(side == yh)
+                def _():
+                    out_ref[r] = total[:, 0:D]
+                    ing_ref[r] = total[:, D : 2 * D]
+
+                @pl.when(side != yh)
+                def _():
+                    fin_s[r] = enc3(total)
+
+            @pl.when(side != yh)
+            def _():
+                fin_move.start()
+
+    over = (((0,), (0,)), ((), ()))
+
+    def wgrad_down():
+        cots = xc[...].reshape(16 * T, D)
+        for ref, width, first in ((ga, FA, 0), (gb, FB, FA)):
+            hidden = ref[:, :, 0:width].reshape(16 * T, width)
+            d_out[first : first + width, :] = lax.dot_general(hidden, cots, over, preferred_element_type=F32)
+
+    def wgrad_in(out, third):
+        for ref, width, first in ((ga, FA, 0), (gb, FB, FA)):
+            grads = ref[:, :, third * width : (third + 1) * width].reshape(16 * T, width)
+            out[:, first : first + width] = dot(ft[...], grads)
 
     gby = gb.at[mate[0]]
     pltpu.make_async_remote_copy(
@@ -440,46 +547,49 @@
             if step < 3:
                 gbz_send(way, step + 1)
         if step == 0:
-            reduce_to_owner(0, 0)
+            send_x(0, 0)
         else:
             for way in range(2):
                 off = offs_of(step - 1)[way]
-                reduce_to_owner(BPOS[off], off)
+                send_x(BPOS[off], off)
+            if step == 1:
+                reduce_x(0)
+            else:
+                for way in range(2):
+                    reduce_x(offs_of(step - 2)[way])
 
     gay_wait(4)
     products(7, 4)
-    keep_ga = pltpu.make_async_copy(ga, ga_hbm, store_sem.at[1])
-    keep_gb = pltpu.make_async_copy(gb, gb_hbm, store_sem.at[2])
-    keep_ga.start()
-    keep_gb.start()
-    reduce_to_owner(7, 4)
-    for k in range(1, 8):
-        col_copy(0, k, at_chip(k)).wait_recv()
-
-        @rows(T)
-        def _(r, k=k):
-            out_ref[r] += dec3(col_r[k, r, 0:D])
-            ing_ref[r] += dec3(col_r[k, r, D : 2 * D])
+    wgrad_down()
+    send_x(7, 4)
+    for way in range(2):
+        reduce_x(offs_of(2)[way])
+    wgrad_in(g_out, 1)
+    reduce_x(4)
+    wgrad_in(u_out, 2)
+    fin_move.wait_recv()
+
+    @rows(T)
+    def _(r):
+        out_ref[r] += dec3(fin_r[r, 0:D])
+        ing_ref[r] += dec3(fin_r[r, D : 2 * D])
 
     for copy in sent:
         copy.wait_send()
 
     @pl.loop(0, NZ)
     def _(at):
-        pltpu.make_async_remote_copy(
-            src_ref=ya_s.at[at], dst_ref=ya_r.at[at], send_sem=ya_ss.at[at], recv_sem=ya_rs.at[at],
-            device_id=mate, device_id_type=MESH,
-        ).wait_send()
+        ya_copy(at, 0).wait_send()
+        ya_copy(at, 1).wait_send()
         sib_copy(at).wait_send()
 
-    for k in range(1, 8):
-        col_copy(0, k, at_chip(k)).wait_send()
-    keep_xc.wait()
-    keep_ga.wait()
-    keep_gb.wait()
-
-
-def layer(features, gate_weight, up_weight, down_weight, cotangent):
+    for side in range(2):
+        for dist in range(1, 4):
+            col_copy(0, side, dist, chip).wait_send()
+    fin_move.wait_send()
+
+
+def layer(*operands):
     vmem = pltpu.VMEM
     dma = pltpu.SemaphoreType.DMA
     hbm = pl.BlockSpec(memory_space=pl.ANY)
@@ -487,19 +597,21 @@
     return pl.pallas_call(
         layer_kernel,
         out_shape=(
-            jax.ShapeDtypeStruct((T, D), F32),
-            jax.ShapeDtypeStruct((T, D), F32),
-            jax.ShapeDtypeStruct((16, 2, T, D), BF16),
-            jax.ShapeDtypeStruct((16, T, CA), BF16),
-            jax.ShapeDtypeStruct((16, T, CB), BF16),
+            vmem((T, D), F32),
+            vmem((T, D), F32),
+            vmem((D, F), F32),
+            vmem((D, F), F32),
+            vmem((F, D), F32),
         ),
         in_specs=[hbm] * 5,
-        out_specs=(full, full, hbm, hbm, hbm),
+        out_specs=(full,) * 5,
         scratch_shapes=[
             vmem((D, F), BF16),
             vmem((D, F), BF16),
             vmem((F, D), BF16),
-            vmem((16, 2, T, D), BF16),
+            vmem((16, T, D), BF16),
+            vmem((16, T, D), BF16),
+            vmem((D, 16 * T), BF16),
             vmem((NZ, 2 * T, CA), F32),
             vmem((NZ, 2 * T, CB), F32),
             vmem((NZ, T, CA), BF16),
@@ -515,56 +627,54 @@
             vmem((NZ, 2, T, 2 * D), F32),
             vmem((NZ, T, 2 * D), F32),
             vmem((NZ, T, 2 * D), BF16),
-            vmem((NZ, T, 2 * D), BF16),
+            vmem((2, 3, T, 2 * D), BF16),
+            vmem((2, T, 2 * D), F32),
+            vmem((T, 2 * D), BF16),
+            vmem((T, 2 * D), BF16),
             dma((5,)),
             dma((8,)), dma((8,)), dma((8,)), dma((8,)),
-            dma((8,)), dma((8,)), dma, dma,
-            dma((2, 4)), dma((2, 4)), dma((2, 4)), dma((2, 4)),
+            dma((8,)), dma((8,)), dma((8,)), dma((8,)),
+            dma((8, 2)), dma((8, 2)), dma, dma,
+            dma((2, 4)), dma((2, 4)), dma((2, 4)), dma((2, 4)), dma((2,)), dma((2,)),
             dma((2, 4)), dma((2, 4)), dma((8,)), dma((8,)),
             dma((2, 4)), dma((2, 4)), dma, dma,
-            dma((8,)), dma((8,)), dma((8,)), dma((8,)),
-            dma((3,)),
+            dma((8,)), dma((8,)), dma((2, 3)), dma((2, 3)), dma, dma,
         ],
         compiler_params=pltpu.CompilerParams(
-            collective_id=0, has_side_effects=True, vmem_limit_bytes=50 * 1024 * 1024
+            collective_id=0, has_side_effects=True, vmem_limit_bytes=48 * 1024 * 1024
         ),
         name="layer",
-    )(features, gate_weight, up_weight, down_weight, cotangent)
-
-
-def wgrad_kernel(xc_ref, ga_ref, gb_ref, g_out, u_out, d_out):
-    tokens = 16 * T
-    over = (((0,), (0,)), ((), ()))
-
-    def product(left, right):
-        return lax.dot_general(left, right, over, preferred_element_type=F32)
-
-    feats = xc_ref[:, 0].reshape(tokens, D)
-    cots = xc_ref[:, 1].reshape(tokens, D)
-    for ref, width, first in ((ga_ref, FA, 0), (gb_ref, FB, FA)):
-        hidden = ref[:, :, 0:width].reshape(tokens, width)
-        d_out[first : first + width, :] = product(hidden, cots)
-        g_out[:, first : first + width] = product(feats, ref[:, :, width : 2 * width].reshape(tokens, width))
-        u_out[:, first : first + width] = product(feats, ref[:, :, 2 * width : 3 * width].reshape(tokens, width))
-
-
-def wgrads(xc, ga, gb):
+    )(*[pltpu.with_memory_space_constraint(operand, pltpu.HBM) for operand in operands])
+
+
+def store_kernel(*refs):
+    sources, targets, sem = refs[:5], refs[5:10], refs[10]
+    copies = []
+    for n in (2, 3, 4, 0, 1):
+        count = 4 if n >= 2 else 1
+        size = sources[n].shape[0] // count
+        for part in range(count):
+            at = pl.ds(part * size, size)
+            copies.append(pltpu.make_async_copy(sources[n].at[at], targets[n].at[at], sem.at[n, part]))
+            copies[-1].start()
+    for copy in copies:
+        copy.wait()
+
+
+def store(*arrays):
     return pl.pallas_call(
-        wgrad_kernel,
-        out_shape=(
-            jax.ShapeDtypeStruct((D, F), F32),
-            jax.ShapeDtypeStruct((D, F), F32),
-            jax.ShapeDtypeStruct((F, D), F32),
-        ),
-        compiler_params=pltpu.CompilerParams(vmem_limit_bytes=50 * 1024 * 1024),
-        name="wgrads",
-    )(xc, ga, gb)
+        store_kernel,
+        out_shape=tuple(pltpu.HBM(array.shape, array.dtype) for array in arrays),
+        in_specs=[pl.BlockSpec(memory_space=pltpu.VMEM)] * 5,
+        out_specs=[pl.BlockSpec(memory_space=pl.ANY)] * 5,
+        scratch_shapes=[pltpu.SemaphoreType.DMA((5, 4))],
+        compiler_params=pltpu.CompilerParams(vmem_limit_bytes=4 * 1024 * 1024),
+        name="store",
+    )(*[pltpu.with_memory_space_constraint(array, pltpu.VMEM) for array in arrays])
 
 
 def body(features, gate_weight, up_weight, down_weight, cotangent):
-    output, input_grad, xc, ga, gb = layer(features, gate_weight, up_weight, down_weight, cotangent)
-    gate_wgrad, up_wgrad, down_wgrad = wgrads(xc, ga, gb)
-    return (output, input_grad, gate_wgrad, up_wgrad, down_wgrad)
+    return store(*layer(features, gate_weight, up_weight, down_weight, cotangent))
 
 
 def solution(mesh):

time: 128 us -> 109 us (0.85)
  Pallas kernels: 118 us -> 108 us
  local copies, waits for them, and re-layouts: 9.28 us -> 0 us
    pallas_call x2, Pallas kernels: 118 us -> 108 us  [the longest x1 105 us: layer(): pl.pallas_call(layer_kernel, out_shape=(vmem((T, D), F32), vmem((T, D), F...]
    unnamed x16 -> x0, local copies, waits for them, and re-layouts: 9.28 us -> none
where the time goes in v2:
time: 109 us
  Pallas kernels  108 us (99%)
    pallas_call x1, Pallas kernels, layer(): pl.pallas_call(layer_kernel, out_shape=(vmem((T, D), F32), vmem((T, D), F...  105 us
    pallas_call x1, Pallas kernels, store(): pl.pallas_call(store_kernel, out_shape=tuple((pltpu.HBM(array.shape, arra...  2.63 us

profile of v2, /device:TPU:4, one launch (start us, length us, event | category | flops | bytes accessed | tf_op | source)
XLA Modules:
  0.0 108.6 jit_solution(10222987865525123324)
XLA Ops:
  0.6 105.4 %layer.1 = (f32[48,512]{1,0:T(8,128)S(1)}, f32[48,512]{1,0:T(8,128)S(1)}, f32[512,896]{1,0:T(8,128)S(1)}, f32[512,896]{1,0:T(8,128)S(1)}, f32[896,512]{1,0:T(8,128)S(1)}) custom-call(bf16[48,512]{1,0:T(8,128)(2,1)} %x_hbm.1, bf16[512,896]{1,0:T(8,128)(2,1)} %g_hbm.1, bf16[512,896]{1,0:T(8,128)(2,1)} %u_hbm.1, bf16[896,512]{1,0:T(8,128)(2,1)} %d_hbm.1, ...), custom_call_target="tpu_custom_call" | custom-call | tf_op jit(solution)/shard_map/layer/pallas_call | solution.py:597
  106.0 2.6 %store.1 = (f32[48,512]{1,0:T(8,128)}, f32[48,512]{1,0:T(8,128)}, f32[512,896]{1,0:T(8,128)}, f32[512,896]{1,0:T(8,128)}, f32[896,512]{1,0:T(8,128)}) custom-call(f32[48,512]{1,0:T(8,128)S(1)} %get-tuple-element.10.refs_0_, f32[48,512]{1,0:T(8,128)S(1)} %get-tuple-element.11.refs_1_, f32[512,896]{1,0:T(8,128)S(1)} %get-tuple-element.12.refs_2_, ...), custom_call_target="tpu_custom_call" | custom-call | tf_op jit(solution)/shard_map/store/pallas_call | solution.py:665

commit v3 on v2

--- a/solution.py
+++ b/solution.py
@@ -68,7 +68,7 @@
     g_w, u_w, d_w, xf, xc, ft, pa, pb, ya_s, ya_r, yb_s, yb_r, za_s, za_r, zb_s, zb_r,
     ga, gb, oi, sib_r, col_s, col_r, acc, fin_s, fin_r,
     load_sem, f_ss, f_rs, c_ss, c_rs, ff_ss, ff_rs, cf_ss, cf_rs, ya_ss, ya_rs, yb_ss, yb_rs,
-    za_ss, za_rs, zb_ss, zb_rs, zh_ss, zh_rs, gaz_ss, gaz_rs, gay_ss, gay_rs, gbz_ss, gbz_rs, gby_ss, gby_rs,
+    za_ss, za_rs, zb_ss, zb_rs, gaz_ss, gaz_rs, gay_ss, gay_rs, gbz_ss, gbz_rs, gby_ss, gby_rs,
     sib_ss, sib_rs, col_ss, col_rs, fin_ss, fin_rs,
 ):
     row, col = lax.axis_index("row"), lax.axis_index("col")
@@ -82,6 +82,9 @@
     def from_chip(k):
         return ((x + 4 - k // 2) % 4) * 2 + (yh + k % 2) % 2
 
+    def place(of_chip):
+        return ((of_chip + 4 * core) % 8) * 2 + core
+
     up_z = ((z + 1) % NZ) * 2 + yl
     down_z = ((z + NZ - 1) % NZ) * 2 + yl
     mate = (z * 2 + 1 - yl, col)
@@ -98,8 +101,8 @@
     sent = []
 
     loads = [
-        pltpu.make_async_copy(x_hbm, xf.at[col], load_sem.at[0]),
-        pltpu.make_async_copy(c_hbm, xc.at[col], load_sem.at[1]),
+        pltpu.make_async_copy(x_hbm, xf.at[place(chip)], load_sem.at[0]),
+        pltpu.make_async_copy(c_hbm, xc.at[place(chip)], load_sem.at[1]),
         pltpu.make_async_copy(g_hbm, g_w, load_sem.at[2]),
         pltpu.make_async_copy(u_hbm, u_w, load_sem.at[3]),
         pltpu.make_async_copy(d_hbm, d_w, load_sem.at[4]),
@@ -124,7 +127,7 @@
     def same_core(k):
         return (row, at_chip(k) * 2 + core)
 
-    mine_f, mine_c = xf.at[col], xc.at[col]
+    mine_f, mine_c = xf.at[place(chip)], xc.at[place(chip)]
     for k in (4, 5, 2, 6, 3, 7, 1):
         sent.append(send(mine_f, mine_f, f_ss.at[k], f_rs.at[k], same_core(k)))
     sent.append(send(mine_f, mine_f, ff_ss.at[0], ff_rs.at[0], sibling))
@@ -133,14 +136,14 @@
     sent.append(send(mine_c, mine_c, cf_ss.at[0], cf_rs.at[0], sibling))
 
     def pass_on(ref, ss, rs, to_ss, to_rs, k):
-        part = ref.at[from_chip(k) * 2 + core]
+        part = ref.at[place(from_chip(k))]
         arrival(part, ss.at[k], rs.at[k]).wait_recv()
         sent.append(send(part, part, to_ss.at[k], to_rs.at[k], sibling))
 
     for k in (1, 2, 6, 3, 7, 4, 5):
         pass_on(xf, f_ss, f_rs, ff_ss, ff_rs, k)
     pass_on(xc, c_ss, c_rs, cf_ss, cf_rs, 1)
-    partner = xc.at[from_chip(1) * 2 + core]
+    partner = xc.at[place(from_chip(1))]
     for k in (5, 3, 7):
         sent.append(send(partner, partner, c_ss.at[k], c_rs.at[k], same_core(k - 1)))
     for copy in loads[2:]:
@@ -175,83 +178,124 @@
         def _(r):
             ya_s[at, r, 2 * FA : CA] = enc5(pa[at, mates(r), 2 * FA : CA])
 
-    YA_COLS = (pl.ds(0, 2 * FA), pl.ds(2 * FA, FA))
-    ZB_COLS = (pl.ds(0, 2 * FB), pl.ds(2 * FB, FB))
+    A_COLS = ((0, 2 * FA), (2 * FA, FA))
+    B_COLS = ((0, 2 * FB), (2 * FB, FB))
 
     def ya_copy(at, which):
-        cols = YA_COLS[which]
+        cols = pl.ds(*A_COLS[which])
         return pltpu.make_async_remote_copy(
             src_ref=ya_s.at[at, :, cols], dst_ref=ya_r.at[at, :, cols],
             send_sem=ya_ss.at[at, which], recv_sem=ya_rs.at[at, which],
             device_id=mate, device_id_type=MESH,
         )
 
-    def ya_wait(at):
-        for which in range(2):
-            ya_copy(at, which).wait_recv()
-
-    def za_part(way, step):
-        if step:
-            return (way, step)
-        return (way, step, slice(None), pl.ds(way * HALF, HALF))
-
-    def za_send(way, step):
-        part = za_part(way, step)
-        copy = send(za_s.at[part], za_r.at[part], za_ss.at[way, step], za_rs.at[way, step], ring[way])
-        sent.append(copy)
-        return copy
-
-    def zb_send(way, step):
-        part = (way, step)
-        copy = send(zb_s.at[part], zb_r.at[part], zb_ss.at[way, step], zb_rs.at[way, step], ring[way])
-        sent.append(copy)
-        return copy
+    def half(which, way):
+        first, width = A_COLS[which]
+        return pl.ds(first + way * (width // 2), width // 2)
+
+    def za_copy(which, way, step):
+        cols = pl.ds(*A_COLS[which]) if step else half(which, way)
+        part = (way, step, slice(None), cols)
+        return pltpu.make_async_remote_copy(
+            src_ref=za_s.at[part], dst_ref=za_r.at[part],
+            send_sem=za_ss.at[which, way, step], recv_sem=za_rs.at[which, way, step],
+            device_id=ring[way], device_id_type=MESH,
+        )
+
+    def zb_copy(which, way, step):
+        tok = slice(None) if step else pl.ds(way * T, T)
+        part = (way, step, tok, pl.ds(*B_COLS[which]))
+        return pltpu.make_async_remote_copy(
+            src_ref=zb_s.at[part], dst_ref=zb_r.at[part],
+            send_sem=zb_ss.at[which, way, step], recv_sem=zb_rs.at[which, way, step],
+            device_id=ring[way], device_id_type=MESH,
+        )
+
+    def za_step(which, step):
+        if step == 0:
+            ya_copy(0, which).wait_recv()
+        for way in range(2):
+            at = POS[4 - step if way == 0 else 4 + step]
+            if step:
+                ya_copy(at, which).wait_recv()
+                za_copy(which, way, step - 1).wait_recv()
+            cols = pl.ds(*A_COLS[which])
+            got, rest = half(which, way), half(which, 1 - way)
+
+            @rows(T)
+            def _(r):
+                if step == 0:
+                    za_s[way, 0, r, got] = enc5(pa[at, r, got] + dec5(ya_r[at, r, got]))
+                elif step == 1:
+                    za_s[way, 1, r, got] = enc5(
+                        pa[at, r, got] + dec5(ya_r[at, r, got]) + dec5(za_r[way, 0, r, got])
+                    )
+                    za_s[way, 1, r, rest] = enc5(pa[at, r, rest] + dec5(ya_r[at, r, rest]))
+                else:
+                    za_s[way, step, r, cols] = enc5(
+                        pa[at, r, cols] + dec5(ya_r[at, r, cols]) + dec5(za_r[way, step - 1, r, cols])
+                    )
+
+            copy = za_copy(which, way, step)
+            copy.start()
+            sent.append(copy)
+
+    def zb_step(which, step):
+        for way in range(2):
+            at = POS[4 - step if way == 0 else 4 + step]
+            if step:
+                zb_copy(which, way, step - 1).wait_recv()
+            cols = pl.ds(*B_COLS[which])
+
+            def shifted(r, by):
+                return pl.ds(pl.multiple_of(r.start + by, 16), 16)
+
+            if step < 2:
+
+                @rows(T)
+                def _(r):
+                    got, rest = shifted(r, way * T), shifted(r, (1 - way) * T)
+                    if step == 0:
+                        zb_s[way, 0, got, cols] = enc5(pb[at, got, cols])
+                    else:
+                        zb_s[way, 1, got, cols] = enc5(pb[at, got, cols] + dec5(zb_r[way, 0, got, cols]))
+                        zb_s[way, 1, rest, cols] = enc5(pb[at, rest, cols])
+            else:
+
+                @rows(2 * T)
+                def _(r):
+                    zb_s[way, step, r, cols] = enc5(pb[at, r, cols] + dec5(zb_r[way, step - 1, r, cols]))
+
+            copy = zb_copy(which, way, step)
+            copy.start()
+            sent.append(copy)
 
     def off_at(at):
         return jnp.where(at % 2 == 1, 4 - (at + 1) // 2, 4 + at // 2)
 
-    zb_moves = {}
-    zh_moves = {}
-
-    def zb_first(which):
-        cols = ZB_COLS[which]
-        for way in range(2):
-            @rows(T)
-            def _(r, way=way):
-                r2 = pl.ds(pl.multiple_of(r.start + way * T, 16), 16)
-                zb_s[way, 0, r2, cols] = enc5(pb[0, r2, cols])
-
-            part = (way, 0, pl.ds(way * T, T), cols)
-            ss, rs = ((zb_ss, zb_rs), (zh_ss, zh_rs))[which]
-            at = (way, 0) if which == 0 else way
-            copy = send(zb_s.at[part], zb_r.at[part], ss.at[at], rs.at[at], ring[way])
-            sent.append(copy)
-            if which == 0:
-                zb_moves[way, 0] = copy
-            else:
-                zh_moves[way] = copy
-
     partial_gu(0, 4)
     ya_copy(0, 0).start()
-    zb_first(0)
+    zb_step(0, 0)
 
     @pl.loop(1, 3)
     def _(at):
         partial_gu(at, off_at(at))
         ya_copy(at, 0).start()
 
-    for k in (2, 6, 4, 3, 7, 5):
-        pass_on(xc, c_ss, c_rs, cf_ss, cf_rs, k)
-
     @pl.loop(3, NZ)
     def _(at):
         partial_gu(at, off_at(at))
 
+    zb_step(0, 1)
+    for k in (2, 6, 4, 3, 7, 5):
+        pass_on(xc, c_ss, c_rs, cf_ss, cf_rs, k)
+    za_step(0, 0)
     for k in range(8):
         arrival(mine_c, cf_ss.at[k], cf_rs.at[k]).wait_recv()
+
     partial_h(0, 4)
     ya_copy(0, 1).start()
-    zb_first(1)
+    zb_step(1, 0)
 
     @pl.loop(1, 3)
     def _(at):
@@ -264,65 +308,21 @@
         ya_copy(at, 0).start()
         ya_copy(at, 1).start()
 
+    zb_step(0, 2)
+    za_step(0, 1)
+    zb_step(1, 1)
+    za_step(1, 0)
+    zb_step(0, 3)
+    zb_step(1, 2)
+    za_step(1, 1)
+    zb_step(1, 3)
     ft[...] = xf[...].reshape(16 * T, D).T
-
-    ya_wait(0)
-    for way in range(2):
-        cols = pl.ds(way * HALF, HALF)
-
-        @rows(T)
-        def _(r, cols=cols, way=way):
-            za_s[way, 0, r, cols] = enc5(pa[0, r, cols] + dec5(ya_r[0, r, cols]))
-
-    za_moves = {(way, 0): za_send(way, 0) for way in range(2)}
-
-    for step in range(1, 4):
+    za_step(0, 2)
+    za_step(1, 2)
+
+    for which in range(2):
         for way in range(2):
-            at = POS[4 - step if way == 0 else 4 + step]
-            zb_moves[way, step - 1].wait_recv()
-            if step == 1:
-                zh_moves[way].wait_recv()
-                got = way * T
-
-                @rows(T)
-                def _(r, got=got, at=at, way=way):
-                    r1 = pl.ds(pl.multiple_of(r.start + got, 16), 16)
-                    zb_s[way, 1, r1] = enc5(pb[at, r1] + dec5(zb_r[way, 0, r1]))
-                    r2 = pl.ds(pl.multiple_of(r.start + (T - got), 16), 16)
-                    zb_s[way, 1, r2] = enc5(pb[at, r2])
-            else:
-
-                @rows(2 * T)
-                def _(r, at=at, way=way, step=step):
-                    zb_s[way, step, r] = enc5(pb[at, r] + dec5(zb_r[way, step - 1, r]))
-
-            zb_moves[way, step] = zb_send(way, step)
-        for way in range(2):
-            at = POS[4 - step if way == 0 else 4 + step]
-            ya_wait(at)
-            za_moves[way, step - 1].wait_recv()
-            if step == 1:
-                got = pl.ds(way * HALF, HALF)
-                rest = pl.ds((1 - way) * HALF, HALF)
-
-                @rows(T)
-                def _(r, got=got, rest=rest, at=at, way=way):
-                    za_s[way, 1, r, got] = enc5(
-                        pa[at, r, got] + dec5(ya_r[at, r, got]) + dec5(za_r[way, 0, r, got])
-                    )
-                    za_s[way, 1, r, rest] = enc5(pa[at, r, rest] + dec5(ya_r[at, r, rest]))
-            else:
-
-                @rows(T)
-                def _(r, at=at, way=way, step=step):
-                    za_s[way, step, r] = enc5(
-                        pa[at, r] + dec5(ya_r[at, r]) + dec5(za_r[way, step - 1, r])
-                    )
-
-            za_moves[way, step] = za_send(way, step)
-
-    for way in range(2):
-        zb_moves[way, 3].wait_recv()
+            zb_copy(which, way, 3).wait_recv()
 
     @rows(T)
     def _(r):
@@ -341,9 +341,12 @@
             (hid * silu).astype(BF16),
         )
 
-    ya_wait(7)
-    for way in range(2):
-        za_moves[way, 3].wait_recv()
+    za_step(0, 3)
+    za_step(1, 3)
+    for which in range(2):
+        ya_copy(7, which).wait_recv()
+        for way in range(2):
+            za_copy(which, way, 3).wait_recv()
 
     @rows(T)
     def _(r):
@@ -432,76 +435,90 @@
             return ref[both, :, first : first + width].reshape(2 * T, width)
 
         outs = dot(part(ga, 0, FA), d_w[0:FA, :]) + dot(part(gb, 0, FB), d_w[FA:F, :])
+        oi[at, :, :, 0:D] = outs.reshape(2, T, D)
+        sib_copy(at, 0).start()
         grads = (
             dot_t(part(ga, FA, FA), g_w[:, 0:FA])
             + dot_t(part(ga, 2 * FA, FA), u_w[:, 0:FA])
             + dot_t(part(gb, FB, FB), g_w[:, FA:F])
             + dot_t(part(gb, 2 * FB, FB), u_w[:, FA:F])
         )
-        oi[at, :, :, 0:D] = outs.reshape(2, T, D)
         oi[at, :, :, D : 2 * D] = grads.reshape(2, T, D)
-        send(oi.at[at, 1 - core], sib_r.at[at], sib_ss.at[at], sib_rs.at[at], sibling)
-
-    def sib_copy(at):
+        sib_copy(at, 1).start()
+
+    OUTS = (pl.ds(0, D), pl.ds(D, D))
+
+    def sib_copy(at, which):
+        cols = OUTS[which]
         return pltpu.make_async_remote_copy(
-            src_ref=oi.at[at, 1 - core], dst_ref=sib_r.at[at], send_sem=sib_ss.at[at], recv_sem=sib_rs.at[at],
+            src_ref=oi.at[at, 1 - core, :, cols], dst_ref=sib_r.at[at, :, cols],
+            send_sem=sib_ss.at[at, which], recv_sem=sib_rs.at[at, which],
             device_id=sibling, device_id_type=MESH,
         )
 
-    def col_copy(at, side, dist, to):
+    def col_copy(at, side, dist, to, which):
+        cols = OUTS[which]
         return pltpu.make_async_remote_copy(
-            src_ref=col_s.at[at], dst_ref=col_r.at[side, dist - 1],
-            send_sem=col_ss.at[side, dist - 1], recv_sem=col_rs.at[side, dist - 1],
+            src_ref=col_s.at[at, :, cols], dst_ref=col_r.at[side, dist - 1, :, cols],
+            send_sem=col_ss.at[side, dist - 1, which], recv_sem=col_rs.at[side, dist - 1, which],
             device_id=(row, to * 2 + core), device_id_type=MESH,
         )
 
-    fin_move = pltpu.make_async_remote_copy(
-        src_ref=fin_s, dst_ref=fin_r, send_sem=fin_ss, recv_sem=fin_rs,
-        device_id=same_core(1), device_id_type=MESH,
-    )
+    def fin_copy(which):
+        cols = OUTS[which]
+        return pltpu.make_async_remote_copy(
+            src_ref=fin_s.at[:, cols], dst_ref=fin_r.at[:, cols], send_sem=fin_ss.at[which],
+            recv_sem=fin_rs.at[which], device_id=same_core(1), device_id_type=MESH,
+        )
 
     def send_x(at, off):
-        piece = (z + off) % NZ
-        to_x, side = piece // 2, piece % 2
-        sib_copy(at).wait_recv()
-
-        @pl.when(to_x == x)
+        owner = (z + off + 4 * core) % NZ
+        to_x, side = owner // 2, owner % 2
+        for which in range(2):
+            cols = OUTS[which]
+            sib_copy(at, which).wait_recv()
+
+            @pl.when(to_x == x)
+            def _():
+                acc[side, :, cols] = oi[at, core, :, cols] + sib_r[at, :, cols]
+
+            @pl.when(to_x != x)
+            def _():
+                @rows(T)
+                def _(r):
+                    col_s[at, r, cols] = enc3(oi[at, core, r, cols] + sib_r[at, r, cols])
+
+                col_copy(at, side, (to_x + 4 - x) % 4, to_x * 2 + yh, which).start()
+
+    def reduce_x(off):
+        owner = (z + off + 4 * core) % NZ
+        side = owner % 2
+
+        @pl.when(owner // 2 == x)
         def _():
-            acc[side] = oi[at, core] + sib_r[at]
-
-        @pl.when(to_x != x)
-        def _():
-            @rows(T)
-            def _(r):
-                col_s[at, r] = enc3(oi[at, core, r] + sib_r[at, r])
-
-            col_copy(at, side, (to_x + 4 - x) % 4, to_x * 2 + yh).start()
-
-    def reduce_x(off):
-        piece = (z + off) % NZ
-        side = piece % 2
-
-        @pl.when(piece // 2 == x)
-        def _():
-            for dist in (1, 3, 2):
-                col_copy(0, side, dist, chip).wait_recv()
-
-            @rows(T)
-            def _(r):
-                total = acc[side, r] + dec3(col_r[side, 0, r]) + dec3(col_r[side, 1, r]) + dec3(col_r[side, 2, r])
-
-                @pl.when(side == yh)
-                def _():
-                    out_ref[r] = total[:, 0:D]
-                    ing_ref[r] = total[:, D : 2 * D]
+            for which in range(2):
+                cols = OUTS[which]
+                for dist in (1, 3, 2):
+                    col_copy(0, side, dist, chip, which).wait_recv()
+
+                @rows(T)
+                def _(r):
+                    total = (
+                        acc[side, r, cols] + dec3(col_r[side, 0, r, cols])
+                        + dec3(col_r[side, 1, r, cols]) + dec3(col_r[side, 2, r, cols])
+                    )
+
+                    @pl.when(side == yh)
+                    def _():
+                        (out_ref, ing_ref)[which][r] = total
+
+                    @pl.when(side != yh)
+                    def _():
+                        fin_s[r, cols] = enc3(total)
 
                 @pl.when(side != yh)
                 def _():
-                    fin_s[r] = enc3(total)
-
-            @pl.when(side != yh)
-            def _():
-                fin_move.start()
+                    fin_copy(which).start()
 
     over = (((0,), (0,)), ((), ()))
 
@@ -542,13 +559,19 @@
                 off = offs_of(step - 1)[way]
                 gay_wait(off)
                 products(BPOS[off], off)
+        if step == 3:
+            for way in range(2):
+                off = offs_of(2)[way]
+                send_x(BPOS[off], off)
+            for way in range(2):
+                reduce_x(offs_of(1)[way])
         for way in range(2):
             gbz_wait(way, step)
             if step < 3:
                 gbz_send(way, step + 1)
         if step == 0:
             send_x(0, 0)
-        else:
+        elif step < 3:
             for way in range(2):
                 off = offs_of(step - 1)[way]
                 send_x(BPOS[off], off)
@@ -560,19 +583,19 @@
 
     gay_wait(4)
     products(7, 4)
-    wgrad_down()
     send_x(7, 4)
     for way in range(2):
         reduce_x(offs_of(2)[way])
+    wgrad_down()
     wgrad_in(g_out, 1)
     reduce_x(4)
     wgrad_in(u_out, 2)
-    fin_move.wait_recv()
-
-    @rows(T)
-    def _(r):
-        out_ref[r] += dec3(fin_r[r, 0:D])
-        ing_ref[r] += dec3(fin_r[r, D : 2 * D])
+    for which in range(2):
+        fin_copy(which).wait_recv()
+
+        @rows(T)
+        def _(r):
+            (out_ref, ing_ref)[which][r] += dec3(fin_r[r, OUTS[which]])
 
     for copy in sent:
         copy.wait_send()
@@ -581,12 +604,15 @@
     def _(at):
         ya_copy(at, 0).wait_send()
         ya_copy(at, 1).wait_send()
-        sib_copy(at).wait_send()
+        sib_copy(at, 0).wait_send()
+        sib_copy(at, 1).wait_send()
 
     for side in range(2):
         for dist in range(1, 4):
-            col_copy(0, side, dist, chip).wait_send()
-    fin_move.wait_send()
+            for which in range(2):
+                col_copy(0, side, dist, chip, which).wait_send()
+    fin_copy(0).wait_send()
+    fin_copy(1).wait_send()
 
 
 def layer(*operands):
@@ -635,10 +661,10 @@
             dma((8,)), dma((8,)), dma((8,)), dma((8,)),
             dma((8,)), dma((8,)), dma((8,)), dma((8,)),
             dma((8, 2)), dma((8, 2)), dma, dma,
-            dma((2, 4)), dma((2, 4)), dma((2, 4)), dma((2, 4)), dma((2,)), dma((2,)),
+            dma((2, 2, 4)), dma((2, 2, 4)), dma((2, 2, 4)), dma((2, 2, 4)),
             dma((2, 4)), dma((2, 4)), dma((8,)), dma((8,)),
             dma((2, 4)), dma((2, 4)), dma, dma,
-            dma((8,)), dma((8,)), dma((2, 3)), dma((2, 3)), dma, dma,
+            dma((8, 2)), dma((8, 2)), dma((2, 3, 2)), dma((2, 3, 2)), dma((2,)), dma((2,)),
         ],
         compiler_params=pltpu.CompilerParams(
             collective_id=0, has_side_effects=True, vmem_limit_bytes=48 * 1024 * 1024

time: 109 us -> 106 us (0.972); the launches traced: 109 us -> 104 us
  Pallas kernels: 108 us -> 104 us
    pallas_call x1, Pallas kernels: 105 us -> 101 us  [layer(): pl.pallas_call(layer_kernel, out_shape=(vmem((T, D), F32), vmem((T, D), F...]
where the time goes in v3:
time: 106 us; the launch traced here: 104 us
  Pallas kernels  104 us (98%)
    pallas_call x1, Pallas kernels, layer(): pl.pallas_call(layer_kernel, out_shape=(vmem((T, D), F32), vmem((T, D), F...  101 us
    pallas_call x1, Pallas kernels, store(): pl.pallas_call(store_kernel, out_shape=tuple((pltpu.HBM(array.shape, arra...  2.63 us

profile of v3, /device:TPU:4, one launch (start us, length us, event | category | flops | bytes accessed | tf_op | source)
XLA Modules:
  0.0 104.3 jit_solution(9981439304142961573)
XLA Ops:
  0.6 101.1 %layer.1 = (f32[48,512]{1,0:T(8,128)S(1)}, f32[48,512]{1,0:T(8,128)S(1)}, f32[512,896]{1,0:T(8,128)S(1)}, f32[512,896]{1,0:T(8,128)S(1)}, f32[896,512]{1,0:T(8,128)S(1)}) custom-call(bf16[48,512]{1,0:T(8,128)(2,1)} %x_hbm.1, bf16[512,896]{1,0:T(8,128)(2,1)} %g_hbm.1, bf16[512,896]{1,0:T(8,128)(2,1)} %u_hbm.1, bf16[896,512]{1,0:T(8,128)(2,1)} %d_hbm.1, ...), custom_call_target="tpu_custom_call" | custom-call | tf_op jit(solution)/shard_map/layer/pallas_call | solution.py:623
  101.7 2.6 %store.1 = (f32[48,512]{1,0:T(8,128)}, f32[48,512]{1,0:T(8,128)}, f32[512,896]{1,0:T(8,128)}, f32[512,896]{1,0:T(8,128)}, f32[896,512]{1,0:T(8,128)}) custom-call(f32[48,512]{1,0:T(8,128)S(1)} %get-tuple-element.10.refs_0_, f32[48,512]{1,0:T(8,128)S(1)} %get-tuple-element.11.refs_1_, f32[512,896]{1,0:T(8,128)S(1)} %get-tuple-element.12.refs_2_, ...), custom_call_target="tpu_custom_call" | custom-call | tf_op jit(solution)/shard_map/store/pallas_call | solution.py:691

commit v4 on v3

--- a/solution.py
+++ b/solution.py
@@ -66,10 +66,10 @@
     x_hbm, g_hbm, u_hbm, d_hbm, c_hbm,
     out_ref, ing_ref, g_out, u_out, d_out,
     g_w, u_w, d_w, xf, xc, ft, pa, pb, ya_s, ya_r, yb_s, yb_r, za_s, za_r, zb_s, zb_r,
-    ga, gb, oi, sib_r, col_s, col_r, acc, fin_s, fin_r,
+    ga, gb, oi, sib_r, col_s, col_r, acc, fin_s, fin_r, last_r,
     load_sem, f_ss, f_rs, c_ss, c_rs, ff_ss, ff_rs, cf_ss, cf_rs, ya_ss, ya_rs, yb_ss, yb_rs,
     za_ss, za_rs, zb_ss, zb_rs, gaz_ss, gaz_rs, gay_ss, gay_rs, gbz_ss, gbz_rs, gby_ss, gby_rs,
-    sib_ss, sib_rs, col_ss, col_rs, fin_ss, fin_rs,
+    sib_ss, sib_rs, col_ss, col_rs, fin_ss, fin_rs, last_ss, last_rs,
 ):
     row, col = lax.axis_index("row"), lax.axis_index("col")
     z, yl = row // 2, row % 2
@@ -519,6 +519,60 @@
                 @pl.when(side != yh)
                 def _():
                     fin_copy(which).start()
+
+    last_owner = (z + 4 + 4 * core) % NZ
+
+    def last_copy(k, to, which):
+        cols = OUTS[which]
+        return pltpu.make_async_remote_copy(
+            src_ref=col_s.at[7, :, cols], dst_ref=last_r.at[k, :, cols],
+            send_sem=last_ss.at[k, which], recv_sem=last_rs.at[k, which],
+            device_id=(row, to * 2 + core), device_id_type=MESH,
+        )
+
+    last_k = ((last_owner // 2 + 4 - x) % 4) * 2 + (last_owner + yh) % 2
+
+    def send_last():
+        for which in range(2):
+            cols = OUTS[which]
+            sib_copy(7, which).wait_recv()
+
+            @pl.when(last_owner == chip)
+            def _():
+                (out_ref, ing_ref)[which][...] = oi[7, core, :, cols] + sib_r[7, :, cols]
+
+            @pl.when(last_owner != chip)
+            def _():
+                @rows(T)
+                def _(r):
+                    col_s[7, r, cols] = enc3(oi[7, core, r, cols] + sib_r[7, r, cols])
+
+                last_copy(last_k, last_owner, which).start()
+
+    def finish():
+        for which in range(2):
+            out = (out_ref, ing_ref)[which]
+            cols = OUTS[which]
+
+            @pl.when(last_owner == chip)
+            def _():
+                for k in range(1, 8):
+                    last_copy(k, chip, which).wait_recv()
+
+                @rows(T)
+                def _(r):
+                    total = out[r]
+                    for k in range(1, 8):
+                        total += dec3(last_r[k, r, cols])
+                    out[r] = total
+
+            @pl.when(last_owner != chip)
+            def _():
+                fin_copy(which).wait_recv()
+
+                @rows(T)
+                def _(r):
+                    out[r] += dec3(fin_r[r, cols])
 
     over = (((0,), (0,)), ((), ()))
 
@@ -583,19 +637,13 @@
 
     gay_wait(4)
     products(7, 4)
-    send_x(7, 4)
+    send_last()
     for way in range(2):
         reduce_x(offs_of(2)[way])
     wgrad_down()
     wgrad_in(g_out, 1)
-    reduce_x(4)
     wgrad_in(u_out, 2)
-    for which in range(2):
-        fin_copy(which).wait_recv()
-
-        @rows(T)
-        def _(r):
-            (out_ref, ing_ref)[which][r] += dec3(fin_r[r, OUTS[which]])
+    finish()
 
     for copy in sent:
         copy.wait_send()
@@ -609,10 +657,22 @@
 
     for side in range(2):
         for dist in range(1, 4):
-            for which in range(2):
-                col_copy(0, side, dist, chip, which).wait_send()
-    fin_copy(0).wait_send()
-    fin_copy(1).wait_send()
+            owner = ((x + dist) % 4) * 2 + side
+
+            @pl.when(owner != last_owner)
+            def _():
+                for which in range(2):
+                    col_copy(0, side, dist, chip, which).wait_send()
+
+    @pl.when(last_owner != chip)
+    def _():
+        for which in range(2):
+            last_copy(last_k, last_owner, which).wait_send()
+
+    @pl.when(last_owner != at_chip(1))
+    def _():
+        for which in range(2):
+            fin_copy(which).wait_send()
 
 
 def layer(*operands):
@@ -657,6 +717,7 @@
             vmem((2, T, 2 * D), F32),
             vmem((T, 2 * D), BF16),
             vmem((T, 2 * D), BF16),
+            vmem((8, T, 2 * D), BF16),
             dma((5,)),
             dma((8,)), dma((8,)), dma((8,)), dma((8,)),
             dma((8,)), dma((8,)), dma((8,)), dma((8,)),
@@ -664,7 +725,7 @@
             dma((2, 2, 4)), dma((2, 2, 4)), dma((2, 2, 4)), dma((2, 2, 4)),
             dma((2, 4)), dma((2, 4)), dma((8,)), dma((8,)),
             dma((2, 4)), dma((2, 4)), dma, dma,
-            dma((8, 2)), dma((8, 2)), dma((2, 3, 2)), dma((2, 3, 2)), dma((2,)), dma((2,)),
+            dma((8, 2)), dma((8, 2)), dma((2, 3, 2)), dma((2, 3, 2)), dma((2,)), dma((2,)), dma((8, 2)), dma((8, 2)),
         ],
         compiler_params=pltpu.CompilerParams(
             collective_id=0, has_side_effects=True, vmem_limit_bytes=48 * 1024 * 1024

time: 106 us -> 105 us (level)
  no operation moved by 1% of the time
where the time goes in v4:
time: 105 us; the launch traced here: 103 us
  Pallas kernels  103 us (98%)
    pallas_call x1, Pallas kernels, layer(): pl.pallas_call(layer_kernel, out_shape=(vmem((T, D), F32), vmem((T, D), F...  100 us
    pallas_call x1, Pallas kernels, store(): pl.pallas_call(store_kernel, out_shape=tuple((pltpu.HBM(array.shape, arra...  2.63 us

profile of v4, /device:TPU:4, one launch (start us, length us, event | category | flops | bytes accessed | tf_op | source)
XLA Modules:
  0.0 103.3 jit_solution(7558523762882319287)
XLA Ops:
  0.6 100.0 %layer.1 = (f32[48,512]{1,0:T(8,128)S(1)}, f32[48,512]{1,0:T(8,128)S(1)}, f32[512,896]{1,0:T(8,128)S(1)}, f32[512,896]{1,0:T(8,128)S(1)}, f32[896,512]{1,0:T(8,128)S(1)}) custom-call(bf16[48,512]{1,0:T(8,128)(2,1)} %x_hbm.1, bf16[512,896]{1,0:T(8,128)(2,1)} %g_hbm.1, bf16[512,896]{1,0:T(8,128)(2,1)} %u_hbm.1, bf16[896,512]{1,0:T(8,128)(2,1)} %d_hbm.1, ...), custom_call_target="tpu_custom_call" | custom-call | tf_op jit(solution)/shard_map/layer/pallas_call | solution.py:683
  100.6 2.6 %store.1 = (f32[48,512]{1,0:T(8,128)}, f32[48,512]{1,0:T(8,128)}, f32[512,896]{1,0:T(8,128)}, f32[512,896]{1,0:T(8,128)}, f32[896,512]{1,0:T(8,128)}) custom-call(f32[48,512]{1,0:T(8,128)S(1)} %get-tuple-element.10.refs_0_, f32[48,512]{1,0:T(8,128)S(1)} %get-tuple-element.11.refs_1_, f32[512,896]{1,0:T(8,128)S(1)} %get-tuple-element.12.refs_2_, ...), custom_call_target="tpu_custom_call" | custom-call | tf_op jit(solution)/shard_map/store/pallas_call | solution.py:752

commit v5 on v4

--- a/solution.py
+++ b/solution.py
@@ -16,6 +16,7 @@
 HALF = CA // 2
 SCALE = 4096.0
 CSCALE = 1024.0
+SMALL = 2.0**-20
 ORDER = (4, 3, 5, 2, 6, 1, 7, 0)
 POS = {off: at for at, off in enumerate(ORDER)}
 BACK = (0, 1, 7, 2, 6, 3, 5, 4)
@@ -36,12 +37,15 @@
 
 def enc3(value):
     value = value * CSCALE
-    return (value * value * value).astype(BF16)
+    size = jnp.abs(value)
+    return (value * jnp.where(size < SMALL, SMALL * SMALL, value * value)).astype(BF16)
 
 
 def dec3(code):
     code = code.astype(F32)
-    root = jnp.exp2(jnp.log2(jnp.abs(code)) * (1.0 / 3.0)) * (1.0 / CSCALE)
+    size = jnp.abs(code)
+    root = jnp.exp2(jnp.log2(size) * (1.0 / 3.0))
+    root = jnp.where(size < SMALL**3, size * (1.0 / SMALL**2), root) * (1.0 / CSCALE)
     return jnp.where(code < 0, -root, root)
 
 

time: 105 us -> 105 us (level)
  no operation moved by 1% of the time
where the time goes in v5:
time: 105 us; the launch traced here: 103 us
  Pallas kernels  103 us (98%)
    pallas_call x1, Pallas kernels, layer(): pl.pallas_call(layer_kernel, out_shape=(vmem((T, D), F32), vmem((T, D), F...  100 us
    pallas_call x1, Pallas kernels, store(): pl.pallas_call(store_kernel, out_shape=tuple((pltpu.HBM(array.shape, arra...  2.63 us

profile of v5, /device:TPU:4, one launch (start us, length us, event | category | flops | bytes accessed | tf_op | source)
XLA Modules:
  0.0 103.4 jit_solution(11892177157664311521)
XLA Ops:
  0.6 100.1 %layer.1 = (f32[48,512]{1,0:T(8,128)S(1)}, f32[48,512]{1,0:T(8,128)S(1)}, f32[512,896]{1,0:T(8,128)S(1)}, f32[512,896]{1,0:T(8,128)S(1)}, f32[896,512]{1,0:T(8,128)S(1)}) custom-call(bf16[48,512]{1,0:T(8,128)(2,1)} %x_hbm.1, bf16[512,896]{1,0:T(8,128)(2,1)} %g_hbm.1, bf16[512,896]{1,0:T(8,128)(2,1)} %u_hbm.1, bf16[896,512]{1,0:T(8,128)(2,1)} %d_hbm.1, ...), custom_call_target="tpu_custom_call" | custom-call | tf_op jit(solution)/shard_map/layer/pallas_call | solution.py:687
  100.7 2.6 %store.1 = (f32[48,512]{1,0:T(8,128)}, f32[48,512]{1,0:T(8,128)}, f32[512,896]{1,0:T(8,128)}, f32[512,896]{1,0:T(8,128)}, f32[896,512]{1,0:T(8,128)}) custom-call(f32[48,512]{1,0:T(8,128)S(1)} %get-tuple-element.10.refs_0_, f32[48,512]{1,0:T(8,128)S(1)} %get-tuple-element.11.refs_1_, f32[512,896]{1,0:T(8,128)S(1)} %get-tuple-element.12.refs_2_, ...), custom_call_target="tpu_custom_call" | custom-call | tf_op jit(solution)/shard_map/store/pallas_call | solution.py:756
